TPU v7x, 256 devices: a whole 4x4x8 slice. The times are simulated.
256 devices in a mesh: lat: 16 (over z, y_hi), lon: 16 (over y_lo, x, core).
Axes of the slice: x: 4, y: 4 (y_hi: 2, y_lo: 2; y = y_hi * 2 + y_lo), z: 8, core: 2. Of those that a mesh axis runs over, the one named last changes fastest.
Arguments:
- saved_state: bfloat16 [256, 1024, 512], P('lat', 'lon'), may hold values from -6 to 6
- cotangent: bfloat16 [256, 1024, 512], P('lat', 'lon'), may hold values from -6 to 6
- row_mask: int32 [256], P('lat'), may hold values from 0 to 1, as said below
- shifts: int32 [2], replicated, may hold values from 1 to 7, as said below
- norm_gain: float32 [512], replicated, may hold values from 0.5 to 1.5
- w_qkv: bfloat16 [512, 1536], replicated, may hold values from -0.25 to 0.25
- w_out: bfloat16 [512, 512], replicated, may hold values from -0.25 to 0.25
- bias_table: float32 [16, 225], replicated, may hold values from -4 to 260
Outputs:
- state_grad: bfloat16 [256, 1024, 512], P('lat', 'lon')
- qkv_grad: float32 [512, 1536], replicated
- out_grad: float32 [512, 512], replicated
- gain_grad: float32 [512], replicated
- bias_grad: float32 [16, 225], replicated
Inputs may be any that keep to these rules, and one draw needn't show every extreme that they name: row_mask is 1 on all rows below some L and 0 from L on, with 224 <= L <= 249. `shifts`: one of the two offsets is 7.
All inputs are finite; a program needn't handle non-finite values.
Results may differ from a plain program's by a relative error of at most 0.013.
Values may be sent and summed in bfloat16 or wider, within the bound.
No kernel may reach another device: no remote copies, remote signals or barrier semaphores. Data moves between devices by JAX's collectives and lax.ppermute only.
A program may use at most 128 MiB of HBM per device.

v0:
```python
import math

import jax
import jax.numpy as jnp
from jax import lax
from jax.sharding import PartitionSpec as P

EPSILON = 1e-05


def shifted(value, axis, steps):
    count = lax.axis_size(axis)
    pairs = [(source, (source + steps) % count) for source in range(count)]
    return lax.ppermute(value, axis, pairs)


def from_behind(array, axis, by):
    count = lax.axis_size(axis)
    pairs = [(i, i + by) for i in range(count) if 0 <= i + by < count]
    return lax.ppermute(array, axis, pairs)


def offsets_table(window):
    cell_count = window * window
    places = jnp.arange(cell_count)
    row_of = places // window
    col_of = places % window
    row_gap = row_of[:, None] - row_of[None, :] + window - 1
    col_gap = col_of[:, None] - col_of[None, :] + window - 1
    flat_gap = (row_gap * (2 * window - 1) + col_gap).reshape(-1)
    entries = jnp.arange((2 * window - 1) ** 2)
    return (flat_gap[:, None] == entries[None, :]).astype(jnp.float32)


def product(pattern, first_op, second_op):
    return jnp.einsum(pattern, first_op, second_op, preferred_element_type=jnp.float32)


def window_backward(tokens, cotangent, live_keys, norm_gain, w_qkv, w_out, bias_table):
    n_win, n_cell, n_chan = tokens.shape
    n_head = bias_table.shape[0]
    head_dim = n_chan // n_head
    window = (math.isqrt(bias_table.shape[1]) + 1) // 2
    onehot = offsets_table(window)
    as_float = tokens.astype(jnp.float32)
    centre_mean = jnp.mean(as_float, -1, keepdims=True)
    centered = as_float - centre_mean
    inv_std = lax.rsqrt(jnp.mean(centered * centered, -1, keepdims=True) + EPSILON)
    x_hat = centered * inv_std
    normed = (x_hat * norm_gain).astype(jnp.bfloat16)
    projected = product("bnc,cd->bnd", normed, w_qkv)
    qk_scale = head_dim ** (-0.5)
    query_heads = (
        (projected[..., :n_chan] * qk_scale)
        .astype(jnp.bfloat16)
        .reshape(n_win, n_cell, n_head, head_dim)
    )
    key_heads = (
        projected[..., n_chan : 2 * n_chan]
        .astype(jnp.bfloat16)
        .reshape(n_win, n_cell, n_head, head_dim)
    )
    value_heads = (
        projected[..., 2 * n_chan :].astype(jnp.bfloat16).reshape(n_win, n_cell, n_head, head_dim)
    )
    bias_full = jnp.dot(bias_table, onehot.T, precision=lax.Precision.HIGHEST).reshape(
        n_head, n_cell, n_cell
    )
    scores = product("bqhd,bkhd->bhqk", query_heads, key_heads) + bias_full[None]
    key_live = live_keys[:, None, None, :] > 0.5
    scores = jnp.where(key_live, scores, -1e30)
    row_max = jnp.max(scores, -1, keepdims=True)
    powers = jnp.exp(scores - row_max)
    attention = powers / jnp.sum(powers, -1, keepdims=True)
    attn_half = attention.astype(jnp.bfloat16)
    mixed = (
        product("bhqk,bkhd->bqhd", attn_half, value_heads)
        .reshape(n_win, n_cell, n_chan)
        .astype(jnp.bfloat16)
    )
    grad_out = (cotangent.astype(jnp.float32) * live_keys[..., None]).astype(jnp.bfloat16)
    out_sum = product("bnc,bne->ce", mixed, grad_out)
    grad_mixed = (
        product("bne,ce->bnc", grad_out, w_out)
        .astype(jnp.bfloat16)
        .reshape(n_win, n_cell, n_head, head_dim)
    )
    grad_attn = product("bqhd,bkhd->bhqk", grad_mixed, value_heads)
    grad_value = product("bhqk,bqhd->bkhd", attn_half, grad_mixed)
    grad_scores = attention * (grad_attn - jnp.sum(attention * grad_attn, -1, keepdims=True))
    bias_sum = jnp.dot(
        jnp.sum(grad_scores, 0).reshape(n_head, n_cell * n_cell),
        onehot,
        precision=lax.Precision.HIGHEST,
    )
    scores_half = grad_scores.astype(jnp.bfloat16)
    grad_query = product("bhqk,bkhd->bqhd", scores_half, key_heads) * qk_scale
    grad_key = product("bhqk,bqhd->bkhd", scores_half, query_heads)
    grad_proj = jnp.concatenate(
        [
            grad_query.reshape(n_win, n_cell, n_chan),
            grad_key.reshape(n_win, n_cell, n_chan),
            grad_value.reshape(n_win, n_cell, n_chan),
        ],
        -1,
    ).astype(jnp.bfloat16)
    qkv_sum = product("bnc,bnd->cd", normed, grad_proj)
    grad_normed = product("bnd,cd->bnc", grad_proj, w_qkv)
    gain_sum = jnp.sum(grad_normed * x_hat, axis=(0, 1))
    grad_hat = grad_normed * norm_gain
    grad_cells = inv_std * (
        grad_hat
        - jnp.mean(grad_hat, -1, keepdims=True)
        - x_hat * jnp.mean(grad_hat * x_hat, -1, keepdims=True)
    )
    return (grad_cells, qkv_sum, out_sum, gain_sum, bias_sum)


def blocks_of(field, window):
    n_rows, n_cols, n_chan = field.shape
    shaped = field.reshape(n_rows // window, window, n_cols // window, window, n_chan)
    return shaped.transpose(0, 2, 1, 3, 4).reshape(
        n_rows // window * (n_cols // window), window * window, n_chan
    )


def grid_of(blocks, n_rows, n_cols, window):
    n_chan = blocks.shape[-1]
    shaped = blocks.reshape(n_rows // window, n_cols // window, window, window, n_chan)
    return shaped.transpose(0, 2, 1, 3, 4).reshape(n_rows, n_cols, n_chan)


def live_of(live_rows, n_cols, window):
    n_rows = live_rows.shape[0]
    spread = jnp.broadcast_to(
        live_rows.reshape(n_rows // window, 1, window, 1),
        (n_rows // window, n_cols // window, window, window),
    )
    return spread.reshape(n_rows // window * (n_cols // window), window * window)


def local(saved_state, cotangent, row_mask, shifts, norm_gain, w_qkv, w_out, bias_table):
    band_rows, cycle_cols, n_chan = saved_state.shape
    window = (math.isqrt(bias_table.shape[1]) + 1) // 2
    shift_lat = shifts[0]
    shift_lon = shifts[1]
    zero_index = shift_lat * 0
    mask_half = row_mask.astype(jnp.bfloat16)
    side_edge = shifted((saved_state[:, -window:], cotangent[:, -window:]), "lon", 1)
    wide_state = jnp.concatenate([side_edge[0], saved_state], 1)
    wide_cot = jnp.concatenate([side_edge[1], cotangent], 1)
    upper_edge = from_behind(
        (wide_state[-window:], wide_cot[-window:], mask_half[-window:]), "lat", 1
    )
    ext_state = jnp.concatenate([upper_edge[0], wide_state], 0)
    ext_cot = jnp.concatenate([upper_edge[1], wide_cot], 0)
    ext_mask = jnp.concatenate([upper_edge[2], mask_half], 0)
    crop_state = lax.dynamic_slice(
        ext_state, (shift_lat, shift_lon, zero_index), (band_rows, cycle_cols, n_chan)
    )
    crop_cot = lax.dynamic_slice(
        ext_cot, (shift_lat, shift_lon, zero_index), (band_rows, cycle_cols, n_chan)
    )
    live_rows = lax.dynamic_slice_in_dim(ext_mask, shift_lat, band_rows).astype(jnp.float32)
    grad_cells, qkv_sum, out_sum, gain_sum, bias_sum = window_backward(
        blocks_of(crop_state, window),
        blocks_of(crop_cot, window),
        live_of(live_rows, cycle_cols, window),
        norm_gain,
        w_qkv,
        w_out,
        bias_table,
    )
    grad_block = grid_of(grad_cells, band_rows, cycle_cols, window)
    ext_grad = jnp.zeros((band_rows + window, cycle_cols + window, n_chan), jnp.float32)
    ext_grad = lax.dynamic_update_slice(ext_grad, grad_block, (shift_lat, shift_lon, zero_index))
    lower_back = from_behind(ext_grad[:window].astype(jnp.bfloat16), "lat", -1).astype(jnp.float32)
    own_rows = ext_grad[window:]
    own_rows = jnp.concatenate([own_rows[:-window], own_rows[-window:] + lower_back], 0)
    side_back = shifted(own_rows[:, :window].astype(jnp.bfloat16), "lon", -1).astype(jnp.float32)
    own_cells = own_rows[:, window:]
    own_cells = jnp.concatenate([own_cells[:, :-window], own_cells[:, -window:] + side_back], 1)
    state_grad = (cotangent.astype(jnp.float32) + own_cells).astype(jnp.bfloat16)
    qkv_total, out_total, gain_total, bias_total = lax.psum(
        (qkv_sum, out_sum, gain_sum, bias_sum), ("lat", "lon")
    )
    norm_factor = 1.0 / math.sqrt(
        band_rows * lax.axis_size("lat") * cycle_cols * lax.axis_size("lon")
    )
    return (
        state_grad,
        qkv_total * norm_factor,
        out_total * norm_factor,
        gain_total * norm_factor,
        bias_total * norm_factor,
    )


def solution(mesh):
    return jax.shard_map(
        local,
        mesh=mesh,
        in_specs=(P("lat", "lon", None), P("lat", "lon", None), P("lat"), P(), P(), P(), P(), P()),
        out_specs=(P("lat", "lon", None), P(), P(), P(), P()),
        check_vma=False,
    )
```

profile of v0, /device:TPU:1, one launch (start us, length us, event | category | flops | bytes accessed | tf_op | source)
XLA Modules:
  0.0 415.9 jit_solution(901755488459530299)
XLA Ops:
  8.3 2.7 collective-permute-start
  11.7 4.8 %collective-permute-start.2 = (bf16[8]{0:T(256)(128)(2,1)S(1)}, bf16[8]{0:T(256)(128)(2,1)S(1)}, u32[]{:S(2)}, u32[]{:S(2)}) collective-permute-start(bf16[8]{0:T(256)(128)(2,1)S(1)} %slice.63), channel_id=1, source_target_pairs={{0,16},{16,32},{32,48},{48,64},{64,80},{80,96},{96,112},{112,128},... | collective-permute-start | bytes 56 | tf_op jit(solution)/shard_map/ppermute | solution.py:20
  17.9 2.7 convolution_bitcast_fusion
  20.7 1.3 fusion.44
  27.3 1.3 constant_dynamic-update-slice_fusion
  30.5 4.1 collective-permute-start.1
  36.0 4.0 collective-permute-start.4
  40.0 6.6 %collective-permute-done.1 = bf16[8,72,512]{2,1,0:T(8,128)(2,1)} collective-permute-done((bf16[8,72,512]{2,1,0:T(8,128)(2,1)}, bf16[8,72,512]{2,1,0:T(8,128)(2,1)}, u32[]{:S(2)}, u32[]{:S(2)}) %collective-permute-start.1) | collective-permute-done | bytes 589856 | tf_op jit(solution)/shard_map/ppermute | solution.py:20
  46.6 1.5 fusion.31
  49.0 1.7 copy.68
  50.8 6.1 %fusion.45 = (bf16[16,64,1536]{2,1,0:T(8,128)(2,1)S(1)}, f32[16,64,1536]{2,1,0:T(8,128)}) fusion(bf16[512,1536]{1,0:T(8,128)(2,1)S(1)} %copy-done, f32[16,64,512]{2,1,0:T(8,128)} %bitcast.81, f32[512]{0:T(512)S(1)} %copy-done.17, f32[16,64]{1,0:T(8,128)S(1)} %div.34, f32[16,64]{1,0:T(8,128)S(1)} %rsqrt.12), kind=kOutput, calls=%fused_computation.98 | convolution fusion | flops 1614282752 | bytes 13117440 | tf_op jit(solution)/shard_map/bnc,cd->bnd/dot_general | solution.py:36
  56.9 1.2 fusion.43
  58.1 1.8 copy.69
  59.9 1.9 fusion.9
  61.7 1.8 copy.70
  63.5 2.7 copy.74
  66.2 1.9 fusion.30
  69.5 1.7 convolution_convert_fusion.1
  71.2 2.8 copy.73
  74.0 9.5 %fusion.46 = (f32[16,16,64]{2,1,0:T(8,128)S(1)}, f32[16,16,64,64]{2,3,1,0:T(8,128)}) fusion(f32[16,64,64]{1,2,0:T(8,128)S(1)} %copy-done.16, pred[16,64]{1,0:T(8,128)(4,1)S(1)} %broadcast_compare_fusion, bf16[16,64,16,32]{1,3,2,0:T(8,128)(2,1)} %bitcast.95, bf16[16,64,16,32]{1,3,2,0:T(8,128)(2,1)} %bitcast.93), kind=kOutput, calls=%fused_computation.99 | convolution fusion | flops 71303232 | bytes 6620160 | tf_op jit(solution)/shard_map/sub | solution.py:73
  83.5 7.1 %multiply_reduce_fusion = (f32[16,16,64]{2,1,0:T(8,128)S(1)}, f32[16,16,64,64]{2,3,1,0:T(8,128)S(1)}) fusion(f32[16,16,64,64]{2,3,1,0:T(8,128)} %get-tuple-element.23, f32[16,16,64]{2,1,0:T(8,128)S(1)} %get-tuple-element.22, bf16[16,64,16,32]{1,3,2,0:T(8,128)(2,1)} %bitcast.103, bf16[16,64,16,32]{1,3,2,0:T(8,128)(2,1)} %bitcast.101), kind=kOutput, calls=%fused_computation.2 | convolution fusion | flops 70238208 | bytes 10616832 | tf_op jit(solution)/shard_map/bqhd,bkhd->bhqk/dot_general | solution.py:36
  90.7 3.3 fusion.6
  94.0 2.5 multiply_convert_fusion
  96.5 3.6 convolution_convert_fusion
  100.2 3.6 fusion.19
  103.8 2.6 fusion.22
  106.4 1.4 fusion.32
  107.7 1.9 copy.78
  109.6 2.7 copy.79
  112.3 2.7 copy.80
  115.0 5.7 %multiply_reduce_fusion.1 = (f32[512]{0:T(512)S(1)}, f32[16,64]{1,0:T(8,128)S(1)}, f32[16,64]{1,0:T(8,128)S(1)}, f32[16,64,512]{2,1,0:T(8,128)}) fusion(f32[16,64,512]{2,1,0:T(8,128)} %bitcast.82, f32[16,64]{1,0:T(8,128)S(1)} %div.34, f32[16,64]{1,0:T(8,128)S(1)} %rsqrt.12, f32[512]{0:T(512)S(1)} %copy-done.17, bf16[512,1536]{1,0:T(8,128)(2,1)S(1)} %copy-done, ...), kind=kOutput, calls=%fused_computation.33 | convolution fusion | flops 1624241664 | bytes 8933376 | tf_op jit(solution)/shard_map/bnd,cd->bnc/dot_general | solution.py:36
  120.7 3.7 convolution_bitcast_fusion.1
  125.4 1.2 reshape.208
  126.7 1.4 copy-done.18
  128.2 1.7 convolution_bitcast_fusion.2
  129.9 2.8 subtract_multiply_fusion.1
  132.8 1.6 copy.81
  134.4 2.2 broadcast_in_dim.21
  136.6 10.6 %dynamic_update_slice.3 = f32[24,72,512]{2,1,0:T(8,128)} dynamic-update-slice(f32[24,72,512]{2,1,0:T(8,128)} %broadcast_in_dim.21, f32[16,64,512]{2,1,0:T(8,128)} %bitcast.90, s32[]{:T(128)S(6)} %select_n.47, s32[]{:T(128)S(6)} %select_n.48, s32[]{:T(128)} %constant.58.clone.1) | dynamic-update-slice | bytes 4194308 | tf_op jit(solution)/shard_map/dynamic_update_slice | solution.py:176
  147.2 1.4 slice.105
  148.6 1.3 collective-permute-start.5
  149.9 1.4 fusion.4
  151.3 92.2 %all-reduce = (f32[512]{0:T(512)S(1)}, f32[16,225]{1,0:T(8,128)S(1)}) all-reduce(f32[512]{0:T(512)S(1)} %get-tuple-element.5, f32[16,225]{1,0:T(8,128)S(1)} %fusion.4), channel_id=1, replica_groups=mesh['lat'=16,'lon'=16] {'lat','lon'}, use_global_device_ids=true, to_apply=%region_10.11 | all-reduce | flops 4112 | bytes 32896 | tf_op jit(solution)/shard_map/psum | solution.py:184
  244.7 1.9 slice_add_fusion
  247.8 3.3 collective-permute-done.6
  251.2 1.3 fusion.10
  252.5 151.6 %all-reduce.4.cloned.1.call-done = (f32[512,1536]{1,0:T(8,128)}, f32[512,512]{1,0:T(8,128)}) async-done(((f32[512,1536]{1,0:T(8,128)}, f32[512,512]{1,0:T(8,128)}), (f32[512,1536]{1,0:T(8,128)}, f32[512,512]{1,0:T(8,128)})) %all-reduce.4.cloned.1.call-update) | async-done | bytes 4194320 | tf_op jit(solution)/shard_map/psum | solution.py:184
  404.1 3.9 broadcast_multiply_fusion
  (89 shorter events, 14.5 us)
Async XLA Ops:
  7.2 43.6 %copy-start = (bf16[512,1536]{1,0:T(8,128)(2,1)S(1)}, bf16[512,1536]{1,0:T(8,128)(2,1)}, u32[]{:S(2)}) copy-start(bf16[512,1536]{1,0:T(8,128)(2,1)} %param.13) | copy-start | bytes 4718596
  7.2 396.9 %all-reduce.4.cloned.1.call-start = ((), (), s32[]{:S(2)}) async-start(), calls=%async_computation | async-start | bytes 8388608 | tf_op jit(solution)/shard_map/psum | solution.py:184
  8.3 19.0 %collective-permute-start = (bf16[16,8,512]{2,1,0:T(8,128)(2,1)S(1)}, bf16[16,8,512]{2,1,0:T(8,128)(2,1)S(1)}, u32[]{:S(2)}, u32[]{:S(2)}) collective-permute-start(bf16[16,8,512]{2,1,0:T(8,128)(2,1)S(1)} %slice.58), channel_id=1, source_target_pairs={{0,1},{1,2},{2,3},{3,4},{4,5},{5,6},{6,7},{7,8},{8,9},{9,10},{10,1... | collective-permute-start | bytes 393224 | tf_op jit(solution)/shard_map/ppermute | solution.py:14
  11.7 15.5 %collective-permute-start.2 = (bf16[8]{0:T(256)(128)(2,1)S(1)}, bf16[8]{0:T(256)(128)(2,1)S(1)}, u32[]{:S(2)}, u32[]{:S(2)}) collective-permute-start(bf16[8]{0:T(256)(128)(2,1)S(1)} %slice.63), channel_id=1, source_target_pairs={{0,16},{16,32},{32,48},{48,64},{64,80},{80,96},{96,112},{112,128},... | collective-permute-start | bytes 56 | tf_op jit(solution)/shard_map/ppermute | solution.py:20
  17.4 17.6 %collective-permute-start.3 = (bf16[16,8,512]{2,1,0:T(8,128)(2,1)S(1)}, bf16[16,8,512]{2,1,0:T(8,128)(2,1)S(1)}, u32[]{:S(2)}, u32[]{:S(2)}) collective-permute-start(bf16[16,8,512]{2,1,0:T(8,128)(2,1)S(1)} %slice.65), channel_id=1, source_target_pairs={{0,1},{1,2},{2,3},{3,4},{4,5},{5,6},{6,7},{7,8},{8,9},{9,10},{10,1... | collective-permute-start | bytes 393224 | tf_op jit(solution)/shard_map/ppermute | solution.py:14
  25.8 9.2 %copy-start.4 = (bf16[16,64,512]{2,1,0:T(8,128)(2,1)S(1)}, bf16[16,64,512]{2,1,0:T(8,128)(2,1)}, u32[]{:S(2)}) copy-start(bf16[16,64,512]{2,1,0:T(8,128)(2,1)} %param.9) | copy-start | bytes 3145732
  28.6 1.0 copy-start.7
  30.5 16.1 %collective-permute-start.1 = (bf16[8,72,512]{2,1,0:T(8,128)(2,1)}, bf16[8,72,512]{2,1,0:T(8,128)(2,1)}, u32[]{:S(2)}, u32[]{:S(2)}) collective-permute-start(bf16[8,72,512]{2,1,0:T(8,128)(2,1)} %slice.74), channel_id=1, source_target_pairs={{0,16},{16,32},{32,48},{48,64},{64,80},{80,96},{96,112},{112,128},... | collective-permute-start | bytes 1769480 | tf_op jit(solution)/shard_map/ppermute | solution.py:20
  35.0 11.7 %copy-start.8 = (bf16[16,72,512]{2,1,0:T(8,128)(2,1)S(1)}, bf16[16,72,512]{2,1,0:T(8,128)(2,1)}, u32[]{:S(2)}) copy-start(bf16[16,72,512]{2,1,0:T(8,128)(2,1)} %copy-done.7) | copy-start | bytes 3538948
  35.1 4.9 %copy-start.9 = (bf16[16,72,512]{2,1,0:T(8,128)(2,1)}, bf16[16,72,512]{2,1,0:T(8,128)(2,1)S(1)}, u32[]{:S(2)}) copy-start(bf16[16,72,512]{2,1,0:T(8,128)(2,1)S(1)} %constant_dynamic-update-slice_fusion.2) | copy-start | bytes 3538948
  36.0 30.3 %collective-permute-start.4 = (bf16[8,72,512]{2,1,0:T(8,128)(2,1)}, bf16[8,72,512]{2,1,0:T(8,128)(2,1)S(1)}, u32[]{:S(2)}, u32[]{:S(2)}) collective-permute-start(bf16[8,72,512]{2,1,0:T(8,128)(2,1)} %slice.77), channel_id=1, source_target_pairs={{0,16},{16,32},{32,48},{48,64},{64,80},{80,96},{96,112},{112,128},... | collective-permute-start | bytes 1769480 | tf_op jit(solution)/shard_map/ppermute | solution.py:20
  48.4 2.4 copy-start.17
  68.4 1.0 copy-start.15
  71.2 2.8 copy-start.16
  83.5 7.1 %slice-start = ((s8[8388608]{0:T(1024)(128)(4,1)}), s8[4194304]{0:T(1024)(128)(4,1)S(1)}, s32[]{:S(2)}) async-start(s8[8388608]{0:T(1024)(128)(4,1)} %bitcast.99), calls=%async_computation.1 | async-start | bytes 8388608
  83.5 7.1 %slice-start.1 = ((s8[8388608]{0:T(1024)(128)(4,1)}), s8[4194304]{0:T(1024)(128)(4,1)S(1)}, s32[]{:S(2)}) async-start(s8[8388608]{0:T(1024)(128)(4,1)} %bitcast.99), calls=%async_computation.2 | async-start | bytes 8388608
  90.6 3.3 copy-start.2
  94.0 2.6 copy-start.3
  96.5 3.6 copy-start.11
  100.2 3.6 copy-start.10
  115.0 5.7 %copy-start.1 = (f32[2,8,8,8,512]{4,3,1,2,0:T(8,128)S(1)}, f32[2,8,8,8,512]{4,3,1,2,0:T(8,128)}, u32[]{:S(2)}) copy-start(f32[2,8,8,8,512]{4,3,1,2,0:T(8,128)} %copy.68) | copy-start | bytes 6291460
  115.0 5.7 %copy-start.12 = (bf16[16,64,512]{2,1,0:T(8,128)(2,1)S(1)}, bf16[16,64,512]{2,1,0:T(8,128)(2,1)}, u32[]{:S(2)}) copy-start(bf16[16,64,512]{2,1,0:T(8,128)(2,1)} %copy.79) | copy-start | bytes 3145732
  115.0 5.7 %copy-start.13 = (bf16[16,64,512]{2,1,0:T(8,128)(2,1)S(1)}, bf16[16,64,512]{2,1,0:T(8,128)(2,1)}, u32[]{:S(2)}) copy-start(bf16[16,64,512]{2,1,0:T(8,128)(2,1)} %copy.80) | copy-start | bytes 3145732
  124.4 2.2 copy-start.6
  126.6 1.6 copy-start.18
  148.6 96.1 %collective-permute-start.5 = (bf16[8,72,512]{2,1,0:T(8,128)(2,1)S(1)}, bf16[8,72,512]{2,1,0:T(8,128)(2,1)S(1)}, u32[]{:S(2)}, u32[]{:S(2)}) collective-permute-start(bf16[8,72,512]{2,1,0:T(8,128)(2,1)S(1)} %slice.105), channel_id=1, source_target_pairs={{16,0},{32,16},{48,32},{64,48},{80,64},{96,80},{112,96},{128,112},... | collective-permute-start | bytes 1769480 | tf_op jit(solution)/shard_map/ppermute | solution.py:20
  246.6 4.5 %collective-permute-start.6 = (bf16[16,8,512]{2,1,0:T(8,128)(2,1)S(1)}, bf16[16,8,512]{2,1,0:T(8,128)(2,1)S(1)}, u32[]{:S(2)}, u32[]{:S(2)}) collective-permute-start(bf16[16,8,512]{2,1,0:T(8,128)(2,1)S(1)} %fusion.39), channel_id=1, source_target_pairs={{0,15},{1,0},{2,1},{3,2},{4,3},{5,4},{6,5},{7,6},{8,7},{9,8},{10,9... | collective-permute-start | bytes 393224 | tf_op jit(solution)/shard_map/ppermute | solution.py:14
  247.8 3.4 copy-start.5
  404.1 3.9 copy-start.14
Sparse Core Ops, SparseCore 0:
  130.1 274.0 all-reduce.3
where the time goes:
time: 418 us; the launch traced here: 416 us
  waiting for transfers between devices  162 us (39%)
  blocking collectives  92.2 us (22%)
  matrix products  52 us (12%)
  local copies, waits for them, and re-layouts  49 us (12%)
  other arithmetic  24.3 us (6%)
  between operations  18.4 us (4%)
  starting transfers between devices  18.3 us (4%)
    psum x1, waiting for transfers between devices, local(): lax.psum((qkv_sum, out_sum, gain_sum, bias_sum), ('lat', 'lon'))  152 us
    psum x1, blocking collectives, local(): lax.psum((qkv_sum, out_sum, gain_sum, bias_sum), ('lat', 'lon'))  92.2 us
    dot_general x10, matrix products, product(): jnp.einsum(pattern, first_op, second_op, preferred_element_type=jnp.float32)  38.4 us
    ppermute x4, starting transfers between devices, from_behind(): return lax.ppermute(array, axis, pairs)  14.3 us
    dynamic_update_slice x1, local copies, waits for them, and re-layouts, local(): lax.dynamic_update_slice(ext_grad, grad_block, (shift_lat, shift_lon, zer...  10.6 us
    sub x1, matrix products, window_backward(): powers = jnp.exp(scores - row_max)  9.53 us
  transfers between devices with their start and end apart: 8, of which 3 were waited for; matrix products, arithmetic and copies ran while one was open for 13% of the time, Pallas kernels for 0%

commit v1 on v0

v1 whole, which is shorter than its diff:
```python
import functools
import math

import jax
import jax.numpy as jnp
from jax import lax
from jax.experimental import pallas as pl
from jax.experimental.pallas import tpu as pltpu
from jax.sharding import PartitionSpec as P

EPSILON = 1e-05


def shifted(value, axis, steps):
    count = lax.axis_size(axis)
    pairs = [(source, (source + steps) % count) for source in range(count)]
    return lax.ppermute(value, axis, pairs)


def from_behind(array, axis, by):
    count = lax.axis_size(axis)
    pairs = [(i, i + by) for i in range(count) if 0 <= i + by < count]
    return lax.ppermute(array, axis, pairs)


def offsets_table(window):
    cell_count = window * window
    places = jnp.arange(cell_count)
    row_of = places // window
    col_of = places % window
    row_gap = row_of[None, :] - row_of[:, None] + window - 1
    col_gap = col_of[None, :] - col_of[:, None] + window - 1
    flat_gap = (row_gap * (2 * window - 1) + col_gap).reshape(-1)
    entries = jnp.arange((2 * window - 1) ** 2)
    return (flat_gap[:, None] == entries[None, :]).astype(jnp.float32)


NT = (((1,), (1,)), ((), ()))
NN = (((1,), (0,)), ((), ()))


def dot(a, b, dims=NN):
    return lax.dot_general(a, b, dims, preferred_element_type=jnp.float32)


def forward_chunk(n_chan, x_ref, go_ref, gain_ref, wt_ref, w_ref, wo_ref, nrm, proj_t, kv, gm_t, scale, base, size):
    rows = pl.ds(base, size)
    x = x_ref[rows].astype(jnp.float32)
    cen = x - jnp.mean(x, -1, keepdims=True)
    inv = lax.rsqrt(jnp.mean(cen * cen, -1, keepdims=True) + EPSILON)
    normed = (cen * inv * gain_ref[...]).astype(jnp.bfloat16)
    nrm[rows] = normed
    proj_t[:n_chan, rows] = (dot(wt_ref[:n_chan], normed, NT) * scale).astype(jnp.bfloat16)
    proj_t[n_chan:, rows] = dot(wt_ref[n_chan:], normed, NT).astype(jnp.bfloat16)
    kv[rows] = dot(normed, w_ref[:, n_chan:]).astype(jnp.bfloat16)
    gm_t[:, rows] = dot(wo_ref[...], go_ref[rows], NT).astype(jnp.bfloat16)


def block_diag(block, step):
    blank = jnp.zeros((step, block.shape[1]), block.dtype)
    count = block.shape[0] // step
    columns = []
    for h in range(count):
        parts = [blank] * count
        parts[h] = block[h * step : (h + 1) * step]
        columns.append(jnp.concatenate(parts, 0))
    return jnp.concatenate(columns, 1)


def attention_unit(n_chan, dim, bias_ref, mask_ref, proj_t, kv, gm_t, mix_t, gp_t, bsum_ref, scale, pair, group, pairs_per_row):
    lanes = pl.ds(pl.multiple_of(pair * 128, 128), 128)
    c0 = pl.multiple_of(group * 128, 128)
    q_t = proj_t[pl.ds(c0, 128), lanes]
    k_t = proj_t[pl.ds(n_chan + c0, 128), lanes]
    v_t = proj_t[pl.ds(2 * n_chan + c0, 128), lanes]
    g_t = gm_t[pl.ds(c0, 128), lanes]
    k_tok = kv[lanes, pl.ds(c0, 128)]
    v_tok = kv[lanes, pl.ds(n_chan + c0, 128)]
    scores = dot(k_tok, block_diag(q_t, dim))
    grads = dot(v_tok, block_diag(g_t, dim))
    first = lax.broadcasted_iota(jnp.int32, (64, 128), 1) < 64
    mask = mask_ref[pair // pairs_per_row]
    heads = 128 // dim
    mixed, dq, dk, dv = [], [], [], []
    for h in range(heads):
        cut = slice(h * 128, (h + 1) * 128)
        rows = slice(h * dim, (h + 1) * dim)
        head = group * heads + h
        s = jnp.where(first, scores[:64, cut], scores[64:, cut]) + bias_ref[head]
        s = s + mask
        e = jnp.exp(s - jnp.max(s, 0, keepdims=True))
        a = e * (1.0 / jnp.sum(e, 0, keepdims=True))
        d = jnp.where(first, grads[:64, cut], grads[64:, cut])
        ad = a * d
        ds = ad - a * jnp.sum(ad, 0, keepdims=True)
        bsum_ref[head] += ds
        zero = jnp.zeros_like(a)
        a2 = jnp.concatenate([jnp.where(first, a, zero), jnp.where(first, zero, a)], 0).astype(jnp.bfloat16)
        ds2 = jnp.concatenate([jnp.where(first, ds, zero), jnp.where(first, zero, ds)], 0).astype(jnp.bfloat16)
        mixed.append(dot(v_t[rows], a2))
        dv.append(dot(g_t[rows], a2, NT))
        dq.append(dot(k_t[rows], ds2) * scale)
        dk.append(dot(q_t[rows], ds2, NT))
    mix_t[pl.ds(c0, 128), lanes] = jnp.concatenate(mixed, 0).astype(jnp.bfloat16)
    gp_t[pl.ds(c0, 128), lanes] = jnp.concatenate(dq, 0).astype(jnp.bfloat16)
    gp_t[pl.ds(n_chan + c0, 128), lanes] = jnp.concatenate(dk, 0).astype(jnp.bfloat16)
    gp_t[pl.ds(2 * n_chan + c0, 128), lanes] = jnp.concatenate(dv, 0).astype(jnp.bfloat16)


def weights_kernel(n_head, pairs_per_row, x_ref, go_ref, bias_ref, mask_ref, gain_ref, wt_ref, w_ref, wo_ref,
                   sums_ref, bsum_ref, gp_t, nrm, proj_t, kv, gm_t, mix_t):
    n_tok, n_chan = x_ref.shape
    dim = n_chan // n_head
    scale = dim ** (-0.5)
    for base in range(0, n_tok, 256):
        forward_chunk(n_chan, x_ref, go_ref, gain_ref, wt_ref, w_ref, wo_ref, nrm, proj_t, kv, gm_t, scale, base, 256)
    bsum_ref[...] = jnp.zeros_like(bsum_ref)
    groups = n_chan // 128

    @pl.loop(0, n_tok // 128 * groups)
    def _(unit):
        attention_unit(n_chan, dim, bias_ref, mask_ref, proj_t, kv, gm_t, mix_t, gp_t, bsum_ref, scale,
                       unit // groups, unit % groups, pairs_per_row)

    for base in range(0, 3 * n_chan, 256):
        sums_ref[base : base + 256] = dot(gp_t[base : base + 256], nrm[...])
    for base in range(0, n_chan, 256):
        sums_ref[3 * n_chan + base : 3 * n_chan + base + 256] = dot(mix_t[base : base + 256], go_ref[...])


def cells_kernel(x_ref, gp_t, gain_ref, w_ref, cells_ref, gsum_ref):
    n_tok, n_chan = x_ref.shape
    total = jnp.zeros((1, n_chan), jnp.float32)
    for base in range(0, n_tok, 256):
        rows = slice(base, base + 256)
        x = x_ref[rows].astype(jnp.float32)
        cen = x - jnp.mean(x, -1, keepdims=True)
        inv = lax.rsqrt(jnp.mean(cen * cen, -1, keepdims=True) + EPSILON)
        x_hat = cen * inv
        grad = dot(w_ref[...], gp_t[:, rows]).T
        total = total + jnp.sum(grad * x_hat, 0, keepdims=True)
        g = grad * gain_ref[...]
        cells_ref[rows] = inv * (g - jnp.mean(g, -1, keepdims=True) - x_hat * jnp.mean(g * x_hat, -1, keepdims=True))
    gsum_ref[...] = total


def window_backward(tokens, grad_out, key_mask, norm_gain, w_qkv, w_out, bias_table):
    n_tok, n_chan = tokens.shape
    n_head = bias_table.shape[0]
    window = (math.isqrt(bias_table.shape[1]) + 1) // 2
    n_cell = window * window
    onehot = offsets_table(window)
    bias = jnp.dot(bias_table, onehot.T, precision=lax.Precision.HIGHEST).reshape(n_head, n_cell, n_cell)
    bias = jnp.concatenate([bias, bias], -1)
    gain = norm_gain.reshape(1, n_chan)
    pairs_per_row = n_tok // 128 // key_mask.shape[0]
    sums, bias_sum, grad_proj = pl.pallas_call(
        functools.partial(weights_kernel, n_head, pairs_per_row),
        out_shape=(
            jax.ShapeDtypeStruct((4 * n_chan, n_chan), jnp.float32),
            jax.ShapeDtypeStruct((n_head, n_cell, 2 * n_cell), jnp.float32),
            jax.ShapeDtypeStruct((3 * n_chan, n_tok), jnp.bfloat16),
        ),
        scratch_shapes=[
            pltpu.VMEM((n_tok, n_chan), jnp.bfloat16),
            pltpu.VMEM((3 * n_chan, n_tok), jnp.bfloat16),
            pltpu.VMEM((n_tok, 2 * n_chan), jnp.bfloat16),
            pltpu.VMEM((n_chan, n_tok), jnp.bfloat16),
            pltpu.VMEM((n_chan, n_tok), jnp.bfloat16),
        ],
        compiler_params=pltpu.CompilerParams(vmem_limit_bytes=48 * 1024 * 1024),
        cost_estimate=pl.CostEstimate(flops=8 * 10**9, bytes_accessed=16 * 2**20, transcendentals=2**20),
        name="weights",
    )(tokens, grad_out, bias, key_mask, gain, w_qkv.T, w_qkv, w_out)
    grad_cells, gain_sum = pl.pallas_call(
        cells_kernel,
        out_shape=(
            jax.ShapeDtypeStruct((n_tok, n_chan), jnp.float32),
            jax.ShapeDtypeStruct((1, n_chan), jnp.float32),
        ),
        compiler_params=pltpu.CompilerParams(vmem_limit_bytes=32 * 1024 * 1024),
        cost_estimate=pl.CostEstimate(flops=16 * 10**8, bytes_accessed=8 * 2**20, transcendentals=0),
        name="cells",
    )(tokens, grad_proj, gain, w_qkv)
    bias_sum = bias_sum[..., :n_cell] + bias_sum[..., n_cell:]
    bias_sum = jnp.dot(bias_sum.reshape(n_head, n_cell * n_cell), onehot, precision=lax.Precision.HIGHEST)
    return grad_cells, sums, gain_sum.reshape(n_chan), bias_sum


def blocks_of(field, window):
    n_rows, n_cols, n_chan = field.shape
    shaped = field.reshape(n_rows // window, window, n_cols // window, window, n_chan)
    return shaped.transpose(0, 2, 1, 3, 4).reshape(n_rows * n_cols, n_chan)


def grid_of(blocks, n_rows, n_cols, window):
    n_chan = blocks.shape[-1]
    shaped = blocks.reshape(n_rows // window, n_cols // window, window, window, n_chan)
    return shaped.transpose(0, 2, 1, 3, 4).reshape(n_rows, n_cols, n_chan)


def total_over_devices(array, axes):
    count = lax.axis_size(axes)
    parts = lax.all_to_all(array.astype(jnp.bfloat16).reshape(count, -1, array.shape[-1]), axes, 0, 0)
    return parts.astype(jnp.float32).sum(0)


def local(saved_state, cotangent, row_mask, shifts, norm_gain, w_qkv, w_out, bias_table):
    band_rows, cycle_cols, n_chan = saved_state.shape
    window = (math.isqrt(bias_table.shape[1]) + 1) // 2
    shift_lat = shifts[0]
    shift_lon = shifts[1]
    zero_index = shift_lat * 0
    mask_half = row_mask.astype(jnp.bfloat16)
    side_edge = shifted((saved_state[:, -window:], cotangent[:, -window:]), "lon", 1)
    wide_state = jnp.concatenate([side_edge[0], saved_state], 1)
    wide_cot = jnp.concatenate([side_edge[1], cotangent], 1)
    upper_edge = from_behind(
        (wide_state[-window:], wide_cot[-window:], mask_half[-window:]), "lat", 1
    )
    ext_state = jnp.concatenate([upper_edge[0], wide_state], 0)
    ext_cot = jnp.concatenate([upper_edge[1], wide_cot], 0)
    ext_mask = jnp.concatenate([upper_edge[2], mask_half], 0)
    crop_state = lax.dynamic_slice(
        ext_state, (shift_lat, shift_lon, zero_index), (band_rows, cycle_cols, n_chan)
    )
    crop_cot = lax.dynamic_slice(
        ext_cot, (shift_lat, shift_lon, zero_index), (band_rows, cycle_cols, n_chan)
    )
    live_rows = lax.dynamic_slice_in_dim(ext_mask, shift_lat, band_rows)
    grad_out = crop_cot * live_rows[:, None, None]
    key_mask = jnp.where(live_rows.astype(jnp.float32) > 0.5, 0.0, -1e30)
    key_mask = jnp.broadcast_to(
        key_mask.reshape(band_rows // window, window, 1, 1), (band_rows // window, window, window, 2 * window * window)
    ).reshape(band_rows // window, window * window, 2 * window * window)
    grad_cells, sums, gain_sum, bias_sum = window_backward(
        blocks_of(crop_state, window),
        blocks_of(grad_out, window),
        key_mask,
        norm_gain,
        w_qkv,
        w_out,
        bias_table,
    )
    grad_block = grid_of(grad_cells, band_rows, cycle_cols, window)
    ext_grad = jnp.zeros((band_rows + window, cycle_cols + window, n_chan), jnp.float32)
    ext_grad = lax.dynamic_update_slice(ext_grad, grad_block, (shift_lat, shift_lon, zero_index))
    lower_back = from_behind(ext_grad[:window].astype(jnp.bfloat16), "lat", -1).astype(jnp.float32)
    own_rows = ext_grad[window:]
    own_rows = jnp.concatenate([own_rows[:-window], own_rows[-window:] + lower_back], 0)
    side_back = shifted(own_rows[:, :window].astype(jnp.bfloat16), "lon", -1).astype(jnp.float32)
    own_cells = own_rows[:, window:]
    own_cells = jnp.concatenate([own_cells[:, :-window], own_cells[:, -window:] + side_back], 1)
    state_grad = (cotangent.astype(jnp.float32) + own_cells).astype(jnp.bfloat16)
    small = jnp.concatenate([gain_sum, bias_sum.reshape(-1)])
    norm_factor = 1.0 / math.sqrt(
        band_rows * lax.axis_size("lat") * cycle_cols * lax.axis_size("lon")
    )
    rest = -small.size % n_chan
    small = jnp.pad(small, (0, rest)).reshape(-1, n_chan)
    part = total_over_devices(total_over_devices(sums, "lon"), "lat")
    part = (part * norm_factor).astype(jnp.bfloat16)
    part = lax.all_gather(lax.all_gather(part, "lat", tiled=True), "lon", tiled=True).astype(jnp.float32)
    small = lax.psum(small, ("lat", "lon")).reshape(-1) * norm_factor
    return (
        state_grad,
        part[: 3 * n_chan].T,
        part[3 * n_chan :],
        small[:n_chan],
        small[n_chan : n_chan + bias_table.size].reshape(bias_table.shape),
    )


def solution(mesh):
    return jax.shard_map(
        local,
        mesh=mesh,
        in_specs=(P("lat", "lon", None), P("lat", "lon", None), P("lat"), P(), P(), P(), P(), P()),
        out_specs=(P("lat", "lon", None), P(), P(), P(), P()),
        check_vma=False,
    )
```

time: 418 us -> 308 us (0.74)
  waiting for transfers between devices: 162 us -> 8.26 us
  blocking collectives: 92.2 us -> 177 us
  matrix products: 52 us -> 3.99 us
  Pallas kernels: 0 us -> 31.7 us
  local copies, waits for them, and re-layouts: 49 us -> 33.6 us
  other arithmetic: 24.3 us -> 14.9 us
    psum x1 -> x0, waiting for transfers between devices: 152 us -> none  [local(): lax.psum((qkv_sum, out_sum, gain_sum, bias_sum), ('lat', 'lon'))]
    all_to_all x0 -> x2, blocking collectives: none -> 57.6 us  [total_over_devices(): lax.all_to_all(array.astype(jnp.bfloat16).reshape(count, -1, array.shape[...]
    dot_general x11 -> x1, matrix products: 39.8 us -> 1.43 us  [window_backward(): jnp.dot(bias_sum.reshape(n_head, n_cell * n_cell), onehot, precision=lax....]
    all_gather x0 -> x1, blocking collectives: none -> 32 us  [local(): lax.all_gather(part, 'lat', tiled=True)]
    pallas_call x0 -> x2, Pallas kernels: none -> 31.7 us  [the longest x1 29.1 us: window_backward(): pl.pallas_call(functools.partial(weights_kernel, n_head, pairs_per_row),...]
    sub x1 -> x0, matrix products: 9.53 us -> none  [window_backward(): powers = jnp.exp(scores - row_max)]
    reshape x4 -> x6, local copies, waits for them, and re-layouts: 8.49 us -> 1.34 us  [the longest x1 0.71 us: local(): small[n_chan:n_chan + bias_table.size].reshape(bias_table.shape)]
    convert_element_type x5 -> x0, local copies, waits for them, and re-layouts: 6.53 us -> none  [the longest x1 2.77 us: window_backward(): grad_mixed = product('bne,ce->bnc', grad_out, w_out).astype(jnp.bfloat16)...]
  transfers between devices with their start and end apart: 8 -> 8, of which waited for: 3 -> 3; matrix products, arithmetic and copies ran while one was open for 13% -> 10% of each run, Pallas kernels for 0% -> 1%
where the time goes in v1:
time: 308 us; the launch traced here: 307 us
  blocking collectives  177 us (57%)
  local copies, waits for them, and re-layouts  33.6 us (11%)
  Pallas kernels  31.7 us (10%)
  starting transfers between devices  19 us (6%)
  between operations  18 us (6%)
  other arithmetic  14.9 us (5%)
  waiting for transfers between devices  8.26 us (3%)
  matrix products  3.99 us (1%)
    psum x1, blocking collectives, local(): small = lax.psum(small, ('lat', 'lon')).reshape(-1) * norm_factor  87.8 us
    all_to_all x2, blocking collectives, total_over_devices(): lax.all_to_all(array.astype(jnp.bfloat16).reshape(count, -1, array.shape[...  57.6 us
    all_gather x1, blocking collectives, local(): lax.all_gather(part, 'lat', tiled=True)  32 us
    pallas_call x1, Pallas kernels, window_backward(): pl.pallas_call(functools.partial(weights_kernel, n_head, pairs_per_row),...  29.1 us
    ppermute x4, starting transfers between devices, from_behind(): return lax.ppermute(array, axis, pairs)  16 us
    dynamic_update_slice x1, local copies, waits for them, and re-layouts, local(): lax.dynamic_update_slice(ext_grad, grad_block, (shift_lat, shift_lon, zer...  10 us
    unnamed x34, local copies, waits for them, and re-layouts  8.71 us
  transfers between devices with their start and end apart: 8, of which 3 were waited for; matrix products, arithmetic and copies ran while one was open for 10% of the time, Pallas kernels for 1%

profile of v1, /device:TPU:1, one launch (start us, length us, event | category | flops | bytes accessed | tf_op | source)
XLA Modules:
  0.0 307.1 jit_solution(4284801528038163507)
XLA Ops:
  7.2 0.7 convert_element_type.38
  7.9 0.7 slice.74
  8.6 6.2 %collective-permute-start.4 = (bf16[8]{0:T(256)(128)(2,1)}, bf16[8]{0:T(256)(128)(2,1)}, u32[]{:S(2)}, u32[]{:S(2)}) collective-permute-start(bf16[8]{0:T(256)(128)(2,1)} %slice.74), channel_id=1, source_target_pairs={{0,16},{16,32},{32,48},{48,64},{64,80},{80,96},{96,112},{112,128},... | collective-permute-start | bytes 56 | tf_op jit(solution)/shard_map/ppermute | solution.py:23
  14.7 0.9 slice.68
  15.6 2.1 collective-permute-start
  17.8 0.9 slice.72
  18.9 0.8 collective-permute-done
  19.7 1.3 constant_dynamic-update-slice_fusion
  21.0 0.9 slice.88
  21.9 3.8 %collective-permute-start.1 = (bf16[8,72,512]{2,1,0:T(8,128)(2,1)}, bf16[8,72,512]{2,1,0:T(8,128)(2,1)}, u32[]{:S(2)}, u32[]{:S(2)}) collective-permute-start(bf16[8,72,512]{2,1,0:T(8,128)(2,1)} %slice.88), channel_id=1, source_target_pairs={{0,16},{16,32},{32,48},{48,64},{64,80},{80,96},{96,112},{112,128},... | collective-permute-start | bytes 1769480 | tf_op jit(solution)/shard_map/ppermute | solution.py:23
  25.8 1.0 copy-done.9
  26.8 0.9 slice.89
  27.7 4.8 %collective-permute-start.3 = (bf16[8,72,512]{2,1,0:T(8,128)(2,1)}, bf16[8,72,512]{2,1,0:T(8,128)(2,1)}, u32[]{:S(2)}, u32[]{:S(2)}) collective-permute-start(bf16[8,72,512]{2,1,0:T(8,128)(2,1)} %slice.89), channel_id=1, source_target_pairs={{0,16},{16,32},{32,48},{48,64},{64,80},{80,96},{96,112},{112,128},... | collective-permute-start | bytes 1769480 | tf_op jit(solution)/shard_map/ppermute | solution.py:23
  32.5 0.6 fusion.11
  35.6 0.6 copy-done.10
  36.2 2.6 convolution_bitcast_fusion
  38.8 0.2 reshape.151
  39.0 1.6 copy.24
  41.8 0.2 pad_maximum_fusion.bias_ref
  42.1 0.7 pad_maximum_fusion.2
  43.1 3.9 %collective-permute-done.3 = bf16[8,72,512]{2,1,0:T(8,128)(2,1)} collective-permute-done((bf16[8,72,512]{2,1,0:T(8,128)(2,1)}, bf16[8,72,512]{2,1,0:T(8,128)(2,1)}, u32[]{:S(2)}, u32[]{:S(2)}) %collective-permute-start.3) | collective-permute-done | bytes 589856 | tf_op jit(solution)/shard_map/ppermute | solution.py:23
  46.9 2.9 fusion.6
  50.2 1.1 copy-done.3
  51.3 29.1 %weights.1 = (f32[2048,512]{1,0:T(8,128)}, f32[16,64,128]{2,1,0:T(8,128)S(1)}, bf16[1536,1024]{1,0:T(8,128)(2,1)}) custom-call(bf16[1024,512]{1,0:T(8,128)(2,1)S(1)} %bitcast.28, bf16[1024,512]{1,0:T(8,128)(2,1)S(1)} %bitcast.30, f32[16,64,128]{2,1,0:T(8,128)S(1)} %pad_maximum_fusion.bias_ref, f32[2,64,128]{2,1,0:T(8,128)S(1)} %broadcast_in_dim.34.mask_ref, ...), custom_call_target="tpu_custom_call" | custom-call | flops 8000000000 | bytes 16777216 | tf_op jit(solution)/shard_map/weights/pallas_call | solution.py:157
  80.4 2.5 convert_element_type.43
  82.9 36.0 %all_to_all.10 = bf16[16,128,512]{2,1,0:T(8,128)(2,1)} all-to-all(bf16[16,128,512]{2,1,0:T(8,128)(2,1)S(1)} %bitcast.34), channel_id=1, replica_groups=mesh['lat'=16,'lon'=16] {'lon'}, dimensions={0} | all-to-all | bytes 4194304 | tf_op jit(solution)/shard_map/all_to_all | solution.py:204
  118.9 2.0 reduce_sum.21
  120.9 21.6 %all_to_all.11 = bf16[16,8,512]{2,1,0:T(8,128)(2,1)S(1)} all-to-all(bf16[16,8,512]{2,1,0:T(8,128)(2,1)S(1)} %bitcast.38), channel_id=1, replica_groups=mesh['lat'=16,'lon'=16] {'lat'}, dimensions={0} | all-to-all | bytes 262144 | tf_op jit(solution)/shard_map/all_to_all | solution.py:204
  142.6 32.0 %all_gather.6 = bf16[128,512]{1,0:T(8,128)(2,1)} all-gather(bf16[8,512]{1,0:T(8,128)(2,1)S(1)} %multiply_convert_fusion), channel_id=1, replica_groups=mesh['lat'=16,'lon'=16] {'lat'}, dimensions={0}, use_global_device_ids=true | all-gather | bytes 139264 | tf_op jit(solution)/shard_map/all_gather | solution.py:263
  174.6 1.9 copy-done.6
  176.5 2.6 cells.1
  179.2 0.2 copy.25
  179.4 2.2 broadcast_in_dim.28
  181.6 10.0 %dynamic_update_slice.3 = f32[24,72,512]{2,1,0:T(8,128)} dynamic-update-slice(f32[24,72,512]{2,1,0:T(8,128)} %broadcast_in_dim.28, f32[16,64,512]{2,1,0:T(8,128)S(1)} %bitcast.35, s32[]{:T(128)S(6)} %select_n.47, s32[]{:T(128)S(6)} %select_n.48, s32[]{:T(128)} %constant.49.clone.1) | dynamic-update-slice | bytes 4194308 | tf_op jit(solution)/shard_map/dynamic_update_slice | solution.py:247
  191.7 1.4 slice.120
  193.0 1.3 collective-permute-start.5
  194.7 1.4 fusion
  196.3 87.8 %psum.7 = f32[9,512]{1,0:T(8,128)S(1)} all-reduce(f32[9,512]{1,0:T(8,128)S(1)} %reshape.160), channel_id=1, replica_groups=mesh['lat'=16,'lon'=16] {'lat','lon'}, use_global_device_ids=true, to_apply=%region_2.3 | all-reduce | flops 4608 | bytes 36864 | tf_op jit(solution)/shard_map/psum | solution.py:264
  284.1 0.6 slice.99
  284.7 0.7 reshape.161
  285.4 1.9 slice_add_fusion
  287.4 0.8 collective-permute-start.6
  288.3 3.5 %collective-permute-done.6 = bf16[16,8,512]{2,1,0:T(8,128)(2,1)S(1)} collective-permute-done((bf16[16,8,512]{2,1,0:T(8,128)(2,1)S(1)}, bf16[16,8,512]{2,1,0:T(8,128)(2,1)S(1)}, u32[]{:S(2)}, u32[]{:S(2)}) %collective-permute-start.6) | collective-permute-done | bytes 131104 | tf_op jit(solution)/shard_map/ppermute | solution.py:17
  291.9 1.3 fusion.1
  293.2 2.2 convert_element_type.46
  295.4 0.3 slice_bitcast_fusion
  295.7 2.4 copy.26
  298.1 2.1 slice.98
  (60 shorter events, 2.0 us)
Async XLA Ops:
  7.2 29.1 %copy-start = (f32[16,225]{1,0:T(8,128)S(1)}, f32[16,225]{1,0:T(8,128)}, u32[]{:S(2)}) copy-start(f32[16,225]{1,0:T(8,128)} %param.15) | copy-start | bytes 43204
  7.2 286.1 %all-gather.2.cloned.1.call-start = ((), (), s32[]{:S(2)}) async-start(), calls=%async_computation.2 | async-start | bytes 2228224 | tf_op jit(solution)/shard_map/all_gather | solution.py:263
  7.9 11.8 %copy-start.13 = (bf16[16]{0:T(256)(128)(2,1)}, bf16[16]{0:T(256)(128)(2,1)S(1)}, u32[]{:S(2)}) copy-start(bf16[16]{0:T(256)(128)(2,1)S(1)} %convert_element_type.38) | copy-start | bytes 100
  8.6 33.5 %collective-permute-start.4 = (bf16[8]{0:T(256)(128)(2,1)}, bf16[8]{0:T(256)(128)(2,1)}, u32[]{:S(2)}, u32[]{:S(2)}) collective-permute-start(bf16[8]{0:T(256)(128)(2,1)} %slice.74), channel_id=1, source_target_pairs={{0,16},{16,32},{32,48},{48,64},{64,80},{80,96},{96,112},{112,128},... | collective-permute-start | bytes 56 | tf_op jit(solution)/shard_map/ppermute | solution.py:23
  15.6 4.1 %collective-permute-start = (bf16[16,8,512]{2,1,0:T(8,128)(2,1)S(1)}, bf16[16,8,512]{2,1,0:T(8,128)(2,1)S(1)}, u32[]{:S(2)}, u32[]{:S(2)}) collective-permute-start(bf16[16,8,512]{2,1,0:T(8,128)(2,1)S(1)} %slice.68), channel_id=1, source_target_pairs={{0,1},{1,2},{2,3},{3,4},{4,5},{5,6},{6,7},{7,8},{8,9},{9,10},{10,1... | collective-permute-start | bytes 393224 | tf_op jit(solution)/shard_map/ppermute | solution.py:17
  18.7 7.0 %collective-permute-start.2 = (bf16[16,8,512]{2,1,0:T(8,128)(2,1)S(1)}, bf16[16,8,512]{2,1,0:T(8,128)(2,1)S(1)}, u32[]{:S(2)}, u32[]{:S(2)}) collective-permute-start(bf16[16,8,512]{2,1,0:T(8,128)(2,1)S(1)} %slice.72), channel_id=1, source_target_pairs={{0,1},{1,2},{2,3},{3,4},{4,5},{5,6},{6,7},{7,8},{8,9},{9,10},{10,1... | collective-permute-start | bytes 393224 | tf_op jit(solution)/shard_map/ppermute | solution.py:17
  18.9 6.8 %copy-start.7 = (bf16[16,64,512]{2,1,0:T(8,128)(2,1)S(1)}, bf16[16,64,512]{2,1,0:T(8,128)(2,1)}, u32[]{:S(2)}) copy-start(bf16[16,64,512]{2,1,0:T(8,128)(2,1)} %param.9) | copy-start | bytes 3145732
  21.9 10.6 %copy-start.12 = (s32[2]{0:T(128)S(1)}, s32[2]{0:T(128)}, u32[]{:S(2)}) copy-start(s32[2]{0:T(128)} %param.11) | copy-start | bytes 28
  21.9 21.2 %collective-permute-start.1 = (bf16[8,72,512]{2,1,0:T(8,128)(2,1)}, bf16[8,72,512]{2,1,0:T(8,128)(2,1)}, u32[]{:S(2)}, u32[]{:S(2)}) collective-permute-start(bf16[8,72,512]{2,1,0:T(8,128)(2,1)} %slice.88), channel_id=1, source_target_pairs={{0,16},{16,32},{32,48},{48,64},{64,80},{80,96},{96,112},{112,128},... | collective-permute-start | bytes 1769480 | tf_op jit(solution)/shard_map/ppermute | solution.py:23
  25.8 1.0 copy-start.9
  26.8 12.2 %copy-start.1 = (bf16[512,1536]{1,0:T(8,128)(2,1)S(1)}, bf16[512,1536]{1,0:T(8,128)(2,1)}, u32[]{:S(2)}) copy-start(bf16[512,1536]{1,0:T(8,128)(2,1)} %w_ref.3) | copy-start | bytes 4718596
  27.7 19.3 %collective-permute-start.3 = (bf16[8,72,512]{2,1,0:T(8,128)(2,1)}, bf16[8,72,512]{2,1,0:T(8,128)(2,1)}, u32[]{:S(2)}, u32[]{:S(2)}) collective-permute-start(bf16[8,72,512]{2,1,0:T(8,128)(2,1)} %slice.89), channel_id=1, source_target_pairs={{0,16},{16,32},{32,48},{48,64},{64,80},{80,96},{96,112},{112,128},... | collective-permute-start | bytes 1769480 | tf_op jit(solution)/shard_map/ppermute | solution.py:23
  35.6 0.6 copy-start.10
  39.0 3.0 copy-start.14
  49.8 1.4 copy-start.3
  49.8 1.5 copy-start.4
  49.8 1.5 copy-start.5
  118.9 55.7 %copy-start.2 = (bf16[512,1536]{1,0:T(8,128)(2,1)S(1)}, bf16[512,1536]{1,0:T(8,128)(2,1)}, u32[]{:S(2)}) copy-start(bf16[512,1536]{1,0:T(8,128)(2,1)} %w_ref.3) | copy-start | bytes 4718596
  174.6 1.9 copy-start.6
  191.6 3.1 copy-start.11
  193.0 92.4 %collective-permute-start.5 = (bf16[8,72,512]{2,1,0:T(8,128)(2,1)S(1)}, bf16[8,72,512]{2,1,0:T(8,128)(2,1)S(1)}, u32[]{:S(2)}, u32[]{:S(2)}) collective-permute-start(bf16[8,72,512]{2,1,0:T(8,128)(2,1)S(1)} %slice.120), channel_id=1, source_target_pairs={{16,0},{32,16},{48,32},{64,48},{80,64},{96,80},{112,96},{128,112},... | collective-permute-start | bytes 1769480 | tf_op jit(solution)/shard_map/ppermute | solution.py:23
  287.4 4.5 %collective-permute-start.6 = (bf16[16,8,512]{2,1,0:T(8,128)(2,1)S(1)}, bf16[16,8,512]{2,1,0:T(8,128)(2,1)S(1)}, u32[]{:S(2)}, u32[]{:S(2)}) collective-permute-start(bf16[16,8,512]{2,1,0:T(8,128)(2,1)S(1)} %fusion.10), channel_id=1, source_target_pairs={{0,15},{1,0},{2,1},{3,2},{4,3},{5,4},{6,5},{7,6},{8,7},{9,8},{10,9... | collective-permute-start | bytes 393224 | tf_op jit(solution)/shard_map/ppermute | solution.py:17
  288.3 3.6 %copy-start.8 = (bf16[16,64,512]{2,1,0:T(8,128)(2,1)S(1)}, bf16[16,64,512]{2,1,0:T(8,128)(2,1)}, u32[]{:S(2)}) copy-start(bf16[16,64,512]{2,1,0:T(8,128)(2,1)} %param.9) | copy-start | bytes 3145732
Sparse Core Ops, SparseCore 0:
  174.7 50.5 all-gather.1

commit v2 on v1

v2 whole, which is shorter than its diff:
```python
import functools
import itertools
import math

import jax
import jax.numpy as jnp
from jax import lax
from jax.experimental import pallas as pl
from jax.experimental.pallas import tpu as pltpu
from jax.sharding import PartitionSpec as P

EPSILON = 1e-05


NT = (((1,), (1,)), ((), ()))
NN = (((1,), (0,)), ((), ()))
LANES = 128
WINDOW = 8
CELLS = WINDOW * WINDOW
TOKENS = 256
MIB = 1024 * 1024


def dot(a, b, dims=NN):
    return lax.dot_general(a, b, dims, preferred_element_type=jnp.float32)


def whole(*_):
    return pl.BlockSpec(memory_space=pltpu.VMEM)


def norm_stats(x):
    cen = x - jnp.mean(x, -1, keepdims=True)
    inv = lax.rsqrt(jnp.mean(cen * cen, -1, keepdims=True) + EPSILON)
    return cen * inv, inv


def project_chunk(n_chan, scale, gain, wt_ref, w_ref, wo_ref, xf, go_ref, nrm_t, proj_t, kv, gm_t, base):
    rows = slice(base, base + TOKENS)
    x_hat, _ = norm_stats(xf[rows])
    normed_f = x_hat * gain
    normed = normed_f.astype(jnp.bfloat16)
    nrm_t[:, rows] = normed_f.T.astype(jnp.bfloat16)
    proj_t[:n_chan, rows] = (dot(wt_ref[:n_chan], normed, NT) * scale).astype(jnp.bfloat16)
    proj_t[n_chan:, rows] = dot(wt_ref[n_chan:], normed, NT).astype(jnp.bfloat16)
    kv[rows] = dot(normed, w_ref[:, n_chan:]).astype(jnp.bfloat16)
    gm_t[:, rows] = dot(wo_ref[...], go_ref[rows], NT).astype(jnp.bfloat16)


def block_diag(block, step):
    blank = jnp.zeros((step, block.shape[1]), block.dtype)
    count = block.shape[0] // step
    columns = []
    for h in range(count):
        parts = [blank] * count
        parts[h] = block[h * step : (h + 1) * step]
        columns.append(jnp.concatenate(parts, 0))
    return jnp.concatenate(columns, 1)


def attention_unit(n_chan, dim, scale, bias_ref, mask, proj_t, kv, gm_t, mix_t, gp_t, bsum_ref, pair, group):
    lanes = pl.ds(pl.multiple_of(pair * LANES, LANES), LANES)
    c0 = pl.multiple_of(group * LANES, LANES)
    q_t = proj_t[pl.ds(c0, LANES), lanes]
    k_t = proj_t[pl.ds(n_chan + c0, LANES), lanes]
    v_t = proj_t[pl.ds(2 * n_chan + c0, LANES), lanes]
    g_t = gm_t[pl.ds(c0, LANES), lanes]
    k_tok = kv[lanes, pl.ds(c0, LANES)]
    v_tok = kv[lanes, pl.ds(n_chan + c0, LANES)]
    scores = dot(k_tok, block_diag(q_t, dim))
    grads = dot(v_tok, block_diag(g_t, dim))
    first = lax.broadcasted_iota(jnp.int32, (CELLS, LANES), 1) < CELLS
    heads = LANES // dim
    mixed, dq, dk, dv = [], [], [], []
    for h in range(heads):
        cut = slice(h * LANES, (h + 1) * LANES)
        rows = slice(h * dim, (h + 1) * dim)
        head = group * heads + h
        s = jnp.where(first, scores[:CELLS, cut], scores[CELLS:, cut]) + bias_ref[head] + mask
        e = jnp.exp(s - jnp.max(s, 0, keepdims=True))
        a = e * (1.0 / jnp.sum(e, 0, keepdims=True))
        d = jnp.where(first, grads[:CELLS, cut], grads[CELLS:, cut])
        ad = a * d
        ds = ad - a * jnp.sum(ad, 0, keepdims=True)
        bsum_ref[head] += ds
        zero = jnp.zeros_like(a)
        a2 = jnp.concatenate([jnp.where(first, a, zero), jnp.where(first, zero, a)], 0).astype(jnp.bfloat16)
        ds2 = jnp.concatenate([jnp.where(first, ds, zero), jnp.where(first, zero, ds)], 0).astype(jnp.bfloat16)
        mixed.append(dot(v_t[rows], a2))
        dv.append(dot(g_t[rows], a2, NT))
        dq.append(dot(k_t[rows], ds2) * scale)
        dk.append(dot(q_t[rows], ds2, NT))
    mix_t[pl.ds(c0, LANES), lanes] = jnp.concatenate(mixed, 0).astype(jnp.bfloat16)
    gp_t[pl.ds(c0, LANES), lanes] = jnp.concatenate(dq, 0).astype(jnp.bfloat16)
    gp_t[pl.ds(n_chan + c0, LANES), lanes] = jnp.concatenate(dk, 0).astype(jnp.bfloat16)
    gp_t[pl.ds(2 * n_chan + c0, LANES), lanes] = jnp.concatenate(dv, 0).astype(jnp.bfloat16)


def place_row(side, own, shift, out, r, live=None):
    line = jnp.concatenate([side.astype(jnp.float32), own.astype(jnp.float32)], 0).reshape(-1, WINDOW, own.shape[1])
    if live is not None:
        line = line * live
    line = pltpu.roll(line, WINDOW - shift, 1)
    head = lax.broadcasted_iota(jnp.int32, line.shape[1:], 0) < WINDOW - shift
    for w in range(line.shape[0] - 1):
        start = w * CELLS + r * WINDOW
        out[start : start + WINDOW] = jnp.where(head, line[w], line[w + 1])


def window_row(n_head, xf, cf, live, gain_ref, wt_ref, w_ref, wo_ref, bias_ref,
               x_out, go_ref, nrm_t, mix_t, gp_t, bsum_ref, proj_t, kv, gm_t):
    n_tok, n_chan = xf.shape
    dim = n_chan // n_head
    scale = dim ** (-0.5)
    x_out[...] = xf[...].astype(jnp.bfloat16)
    go_ref[...] = cf[...].astype(jnp.bfloat16)
    for base in range(0, n_tok, TOKENS):
        project_chunk(n_chan, scale, gain_ref[...], wt_ref, w_ref, wo_ref, xf, go_ref, nrm_t, proj_t, kv, gm_t, base)
    mask = jnp.concatenate(
        [jnp.broadcast_to((live[r] - 1.0) * 1e30, (WINDOW, LANES)) for r in range(WINDOW)], 0
    )
    groups = n_chan // LANES

    @pl.loop(0, n_tok // LANES * groups)
    def _(unit):
        attention_unit(n_chan, dim, scale, bias_ref, mask, proj_t, kv, gm_t, mix_t, gp_t, bsum_ref,
                       unit // groups, unit % groups)


def inner_kernel(n_head, meta, x_ref, cot_ref, side_ref, bias_ref, gain_ref, wt_ref, w_ref, wo_ref,
                 x_out, go_ref, nrm_t, mix_t, gp_t, bsum_ref, xf, cf, proj_t, kv, gm_t):
    lat, lon = meta[0], meta[1]
    live = []
    for r in range(WINDOW):
        live.append(meta[5 + WINDOW + lat + r].astype(jnp.float32))
        place_row(side_ref[0, lat + r], x_ref[lat + r], lon, xf, r)
        place_row(side_ref[1, lat + r], cot_ref[lat + r], lon, cf, r, live[r])
    bsum_ref[...] = jnp.zeros_like(bsum_ref)
    window_row(n_head, xf, cf, live, gain_ref, wt_ref, w_ref, wo_ref, bias_ref,
               x_out, go_ref, nrm_t, mix_t, gp_t, bsum_ref, proj_t, kv, gm_t)


def outer_kernel(n_head, counts, meta, x_ref, cot_ref, side_ref, top_ref, corner_ref, bias_ref, gain_ref, wt_ref, w_ref, wo_ref,
                 go_in, nrm_in, mix_in, gp_in, bsum_in,
                 x_out, gp_t, keep_ref, send_ref,
                 go_ref, nrm_t, mix_t, bsum_ref, xf, cf, proj_t, kv, gm_t, sums, spread_a, spread_b):
    n_chan = gain_ref.shape[1]
    lat, lon = meta[0], meta[1]
    live = []
    for r in range(WINDOW):
        e = lat + r
        above = e < WINDOW
        up = jnp.minimum(e, WINDOW - 1)
        own = jnp.maximum(e - WINDOW, 0)
        live.append(meta[5 + e].astype(jnp.float32))
        side = [jnp.where(above, corner_ref[k, up], side_ref[k, own]) for k in range(2)]
        place_row(side[0], jnp.where(above, top_ref[0, up], x_ref[own]), lon, xf, r)
        place_row(side[1], jnp.where(above, top_ref[1, up], cot_ref[own]), lon, cf, r, live[r])
    bsum_ref[...] = bsum_in[...]
    window_row(n_head, xf, cf, live, gain_ref, wt_ref, w_ref, wo_ref, bias_ref,
               x_out, go_ref, nrm_t, mix_t, gp_t, bsum_ref, proj_t, kv, gm_t)

    n_proj = 3 * n_chan
    gain_sum = jnp.zeros((n_chan, 1), jnp.float32)
    for base in range(0, n_proj, TOKENS):
        cols = slice(base, base + TOKENS)
        part = dot(nrm_in[...], gp_in[cols], NT) + dot(nrm_t[...], gp_t[cols], NT)
        sums[:, cols] = part
        gain_sum += jnp.sum(part * w_ref[:, cols].astype(jnp.float32), 1, keepdims=True)
    for base in range(0, n_chan, TOKENS):
        cols = slice(base, base + TOKENS)
        sums[:, n_proj + base : n_proj + base + TOKENS] = dot(mix_in[...], go_in[:, cols]) + dot(mix_t[...], go_ref[:, cols])

    width = 2 * LANES
    cell = lax.broadcasted_iota(jnp.int32, (LANES, width), 0) % CELLS
    lane = lax.broadcasted_iota(jnp.int32, (LANES, width), 1)
    place = (cell // WINDOW) * 16 + cell % WINDOW + 119
    onehot = (lane == place).astype(jnp.float32).astype(jnp.bfloat16)
    flat = bsum_ref[...].reshape(n_head * CELLS, LANES)
    high = flat.astype(jnp.bfloat16)
    low = (flat - high.astype(jnp.float32)).astype(jnp.bfloat16)
    spread = dot(high, onehot) + dot(low, onehot)
    spread_a[...] = spread[:, :LANES]
    spread_b[...] = spread[:, LANES:]
    bias_sum = jnp.zeros((n_head, width), jnp.float32)
    for j in range(CELLS):
        row = jnp.concatenate([ref[pl.ds(j, n_head, stride=CELLS), :] for ref in (spread_a, spread_b)], 1)
        by = (j // WINDOW) * 16 + j % WINDOW
        bias_sum += pltpu.roll(row, width - by, 1) if by else row
    tail = lax.broadcasted_iota(jnp.int32, (n_chan, LANES), 1) == LANES - 1
    bias_rows = jnp.concatenate(
        [bias_sum[:, :LANES], bias_sum[:, LANES:], jnp.zeros((n_chan - 2 * n_head, LANES), jnp.float32)], 0
    )
    sums[:, n_proj + n_chan :] = jnp.where(tail, gain_sum * (1.0 / gain_col(gain_ref)), bias_rows)

    n_c, n_x, n_y = counts
    rows = n_chan // (n_c * n_x * n_y)
    for c in range(n_c):
        for x in range(n_x):
            for y in range(n_y):
                chunk = sums[((c * n_x + x) * n_y + y) * rows : ((c * n_x + x) * n_y + y + 1) * rows]
                at = lax.rem(x - meta[3] + n_x, n_x) * n_y + lax.rem(y - meta[4] + n_y, n_y)

                @pl.when(meta[2] == c)
                def _():
                    keep_ref[at] = chunk

                @pl.when(meta[2] != c)
                def _():
                    send_ref[at] = chunk.astype(jnp.bfloat16)


def gain_col(gain_ref):
    n_chan = gain_ref.shape[1]
    return jnp.broadcast_to(gain_ref[...], (LANES, n_chan)).T[:, :1]


def cells_kernel(meta, xa_ref, xb_ref, gpa_ref, gpb_ref, cot_ref, gain_ref, w_ref, base_ref, top_ref, side_ref, ext):
    n_rows, n_cols, n_chan = cot_ref.shape
    lat, lon = meta[0], meta[1]
    ext[...] = jnp.zeros_like(ext)
    for part, (x_ref, gp_t) in enumerate(((xb_ref, gpb_ref), (xa_ref, gpa_ref))):
        n_tok = x_ref.shape[0]
        cells = []
        for base in range(0, n_tok, TOKENS):
            rows = slice(base, base + TOKENS)
            x_hat, inv = norm_stats(x_ref[rows].astype(jnp.float32))
            g = dot(w_ref[...], gp_t[:, rows]).T * gain_ref[...]
            cells.append(inv * (g - jnp.mean(g, -1, keepdims=True) - x_hat * jnp.mean(g * x_hat, -1, keepdims=True)))
        blank = jnp.zeros((1, WINDOW, n_chan), jnp.float32)
        head = lax.broadcasted_iota(jnp.int32, (WINDOW, n_chan), 0) < lon
        for r in range(WINDOW):
            row = jnp.stack(
                [
                    cells[w * CELLS // TOKENS][w * CELLS % TOKENS + r * WINDOW :][:WINDOW]
                    for w in range(n_tok // CELLS)
                ],
                0,
            )
            row = jnp.concatenate([blank, pltpu.roll(row, lon, 1), blank], 0)
            for t in range(row.shape[0] - 1):
                ext[lat + part * WINDOW + r, t * WINDOW : (t + 1) * WINDOW, :] = jnp.where(head, row[t], row[t + 1])
    for r in range(n_rows):
        base_ref[r] = (cot_ref[r].astype(jnp.float32) + ext[WINDOW + r, WINDOW:]).astype(jnp.bfloat16)
        side_ref[r] = ext[WINDOW + r, :WINDOW].astype(jnp.bfloat16)
    top_ref[...] = ext[:WINDOW].astype(jnp.bfloat16)


def first_add_kernel(keep_ref, got_ref, own_ref, *send_refs):
    size = own_ref.shape[0]
    for k in range(len(send_refs) + 1):
        cut = slice(k * size, (k + 1) * size)
        total = keep_ref[cut] + got_ref[cut].astype(jnp.float32)
        if k:
            send_refs[k - 1][...] = total.astype(jnp.bfloat16)
        else:
            own_ref[...] = total


def next_add_kernel(n_got, own_ref, *refs):
    got, out_ref, send_refs = refs[:n_got], refs[n_got], refs[n_got + 1 :]
    size = out_ref.shape[0]
    for k in range(len(send_refs) + 1):
        cut = slice(k * size, (k + 1) * size)
        total = own_ref[cut]
        for ref in got:
            total = total + ref[cut].astype(jnp.float32)
        if k:
            send_refs[k - 1][...] = total.astype(jnp.bfloat16)
        else:
            out_ref[...] = total.astype(out_ref.dtype)


def unpack_kernel(counts, n_proj, factor, meta, mine_ref, other_ref, qkv_ref, out_ref, small_ref):
    n_c, n_x, n_y = counts
    rows = mine_ref.shape[1]
    n_chan = out_ref.shape[1]
    for c in range(n_c):
        for x in range(n_x):
            for y in range(n_y):
                at = lax.rem(x - meta[3] + n_x, n_x) * n_y + lax.rem(y - meta[4] + n_y, n_y)
                chunk = jnp.where(meta[2] == c, mine_ref[at], other_ref[at]).astype(jnp.float32) * factor
                to = slice(((c * n_x + x) * n_y + y) * rows, ((c * n_x + x) * n_y + y + 1) * rows)
                qkv_ref[to] = chunk[:, :n_proj]
                out_ref[to] = chunk[:, n_proj : n_proj + n_chan]
                small_ref[to] = chunk[:, n_proj + n_chan :]


class Places:
    def __init__(self):
        self.n_lat, self.n_lon = lax.axis_size("lat"), lax.axis_size("lon")
        self.c = 2
        self.x = min(4, self.n_lon // self.c)
        self.y_low = self.n_lon // (self.c * self.x)
        self.y_high = 2
        self.y = self.y_low * self.y_high
        self.z = self.n_lat // self.y_high

    def index(self, z, y, x, c):
        high, low = divmod(y, self.y_low)
        return (z * self.y_high + high) * self.n_lon + (low * self.x + x) * self.c + c

    def mine(self):
        lat, lon = lax.axis_index("lat"), lax.axis_index("lon")
        return (
            lon % self.c,
            lon // self.c % self.x,
            lat % self.y_high * self.y_low + lon // (self.c * self.x),
        )

    def move(self, array, to):
        every = itertools.product(range(self.z), range(self.y), range(self.x), range(self.c))
        pairs = [(self.index(*at), self.index(*to(*at))) for at in every]
        return lax.ppermute(array, ("lat", "lon"), pairs)

    def by_c(self, array):
        return self.move(array, lambda z, y, x, c: (z, y, x, 1 - c))

    def by_x(self, array, k):
        return self.move(array, lambda z, y, x, c: (z, y, (x + k) % self.x, c))

    def by_y(self, array, k):
        return self.move(array, lambda z, y, x, c: (z, (y + k) % self.y, x, c))

    def by_z(self, array, bits):
        return self.move(array, lambda z, y, x, c: (z ^ bits, y, x, c))


def small_call(kernel, outs, name, *args):
    return pl.pallas_call(
        kernel,
        out_shape=outs,
        compiler_params=pltpu.CompilerParams(vmem_limit_bytes=32 * MIB),
        name=name,
    )(*args)


def total_over_devices(places, keep, send):
    shape = keep.shape[1:]
    bf = functools.partial(jax.ShapeDtypeStruct, dtype=jnp.bfloat16)
    got = places.by_c(send)
    own = jax.ShapeDtypeStruct((places.y, *shape), jnp.float32)
    own, *sends = small_call(first_add_kernel, (own,) + (bf((places.y, *shape)),) * (places.x - 1), "add_c", keep, got)
    got = [places.by_x(part, k + 1) for k, part in enumerate(sends)]
    nxt = jax.ShapeDtypeStruct((1, *shape), jnp.float32)
    own, *sends = small_call(
        functools.partial(next_add_kernel, len(got)), (nxt,) + (bf((1, *shape)),) * (places.y - 1), "add_x", own, *got
    )
    got = [places.by_y(part, k + 1) for k, part in enumerate(sends)]
    (mine,) = small_call(functools.partial(next_add_kernel, len(got)), (bf((1, *shape)),), "add_y", own, *got)
    for bits in {1: (), 2: (1,), 4: (1, 3), 8: (1, 2, 6)}[places.z]:
        other = places.by_z(mine, bits)
        mine = (mine.astype(jnp.float32) + other.astype(jnp.float32)).astype(jnp.bfloat16)
    mine = jnp.concatenate([mine] + [places.by_y(mine, -k) for k in range(1, places.y)], 0)
    mine = jnp.concatenate([mine] + [places.by_x(mine, -k) for k in range(1, places.x)], 0)
    return mine, places.by_c(mine)


def ring(array, lat, lon):
    n_lat, n_lon = lax.axis_size("lat"), lax.axis_size("lon")
    pairs = [
        (i * n_lon + j, (i + lat) % n_lat * n_lon + (j + lon) % n_lon) for i in range(n_lat) for j in range(n_lon)
    ]
    return lax.ppermute(array, ("lat", "lon"), pairs)


def bias_of_pairs(bias_table):
    places = jnp.arange(CELLS)
    row_of, col_of = places // WINDOW, places % WINDOW
    row_gap = row_of[None, :] - row_of[:, None] + WINDOW - 1
    col_gap = col_of[None, :] - col_of[:, None] + WINDOW - 1
    gap = (row_gap * (2 * WINDOW - 1) + col_gap).reshape(-1)
    onehot = (jnp.arange(bias_table.shape[1])[:, None] == gap[None, :]).astype(jnp.float32)
    full = jnp.dot(bias_table, onehot, precision=lax.Precision.HIGHEST).reshape(-1, CELLS, CELLS)
    return jnp.concatenate([full, full], -1)


def local(saved_state, cotangent, row_mask, shifts, norm_gain, w_qkv, w_out, bias_table):
    n_rows, n_cols, n_chan = saved_state.shape
    n_head = bias_table.shape[0]
    n_proj = w_qkv.shape[1]
    n_tok = n_rows // 2 * n_cols
    places = Places()
    counts = (places.c, places.x, places.y)
    bf, f32 = jnp.bfloat16, jnp.float32

    side = ring(jnp.stack([saved_state[:, -WINDOW:], cotangent[:, -WINDOW:]]), 0, 1)
    top = ring(jnp.stack([saved_state[-WINDOW:], cotangent[-WINDOW:]]), 1, 0)
    mask_block = jnp.broadcast_to(row_mask[-WINDOW:, None, None].astype(bf), (WINDOW, WINDOW, n_chan))
    corner = ring(
        jnp.stack([saved_state[-WINDOW:, -WINDOW:], cotangent[-WINDOW:, -WINDOW:], mask_block]), 1, 1
    )
    at = jnp.stack(places.mine()).astype(jnp.int32)
    bias = bias_of_pairs(bias_table)
    gain = norm_gain.reshape(1, n_chan)
    w_t = w_qkv.T

    smem = pl.BlockSpec(memory_space=pltpu.SMEM)
    tile = functools.partial(jax.ShapeDtypeStruct, dtype=bf)
    work = [
        pltpu.VMEM((n_tok, n_chan), f32),
        pltpu.VMEM((n_tok, n_chan), f32),
        pltpu.VMEM((n_proj, n_tok), bf),
        pltpu.VMEM((n_tok, 2 * n_chan), bf),
        pltpu.VMEM((n_chan, n_tok), bf),
    ]
    meta_inner = jnp.concatenate([shifts, at, jnp.zeros((WINDOW,), jnp.int32), row_mask])
    x_in, go_in, nrm_in, mix_in, gp_in, bsum_in = pl.pallas_call(
        functools.partial(inner_kernel, n_head),
        out_shape=(
            tile((n_tok, n_chan)),
            tile((n_tok, n_chan)),
            tile((n_chan, n_tok)),
            tile((n_chan, n_tok)),
            tile((n_proj, n_tok)),
            jax.ShapeDtypeStruct((n_head, CELLS, LANES), f32),
        ),
        in_specs=[smem] + [whole()] * 8,
        scratch_shapes=work,
        compiler_params=pltpu.CompilerParams(vmem_limit_bytes=40 * MIB),
        cost_estimate=pl.CostEstimate(flops=8 * 10**9, bytes_accessed=16 * MIB, transcendentals=2**19),
        name="inner",
    )(meta_inner, saved_state, cotangent, side, bias, gain, w_t, w_qkv, w_out)

    above = jnp.where(lax.axis_index("lat") > 0, corner[2, :, 0, 0].astype(jnp.int32), 0)
    meta = jnp.concatenate([shifts, at, above, row_mask])
    width = n_proj + n_chan + LANES
    rows = n_chan // math.prod(counts)
    half = math.prod(counts) // 2
    x_out, gp_out, keep, send = pl.pallas_call(
        functools.partial(outer_kernel, n_head, counts),
        out_shape=(
            tile((n_tok, n_chan)),
            tile((n_proj, n_tok)),
            jax.ShapeDtypeStruct((half, rows, width), f32),
            tile((half, rows, width)),
        ),
        in_specs=[smem] + [whole()] * 15,
        scratch_shapes=[
            pltpu.VMEM((n_tok, n_chan), bf),
            pltpu.VMEM((n_chan, n_tok), bf),
            pltpu.VMEM((n_chan, n_tok), bf),
            pltpu.VMEM((n_head, CELLS, LANES), f32),
            *work,
            pltpu.VMEM((n_chan, width), f32),
            pltpu.VMEM((n_head * CELLS, LANES), f32),
            pltpu.VMEM((n_head * CELLS, LANES), f32),
        ],
        compiler_params=pltpu.CompilerParams(vmem_limit_bytes=56 * MIB),
        cost_estimate=pl.CostEstimate(flops=10**10, bytes_accessed=24 * MIB, transcendentals=2**19),
        name="outer",
    )(meta, saved_state, cotangent, side, top, corner, bias, gain, w_t, w_qkv, w_out, go_in, nrm_in, mix_in, gp_in, bsum_in)

    mine, other = total_over_devices(places, keep, send)

    base, top_grad, side_grad = pl.pallas_call(
        cells_kernel,
        out_shape=(
            tile((n_rows, n_cols, n_chan)),
            tile((WINDOW, n_cols + WINDOW, n_chan)),
            tile((n_rows, WINDOW, n_chan)),
        ),
        in_specs=[smem] + [whole()] * 7,
        scratch_shapes=[pltpu.VMEM((n_rows + WINDOW, n_cols + WINDOW, n_chan), f32)],
        compiler_params=pltpu.CompilerParams(vmem_limit_bytes=40 * MIB),
        cost_estimate=pl.CostEstimate(flops=16 * 10**8, bytes_accessed=12 * MIB, transcendentals=0),
        name="cells",
    )(meta, x_in, x_out, gp_in, gp_out, cotangent, gain, w_qkv)
    top_grad = ring(top_grad, -1, 0)
    side_grad = jnp.concatenate([side_grad[:-WINDOW], side_grad[-WINDOW:] + top_grad[:, :WINDOW]], 0)
    side_grad = ring(side_grad, 0, -1)
    edge = jnp.pad(top_grad[:, WINDOW:], ((n_rows - WINDOW, 0), (0, 0), (0, 0)))
    edge = edge + jnp.pad(side_grad, ((0, 0), (n_cols - WINDOW, 0), (0, 0)))
    state_grad = (base.astype(f32) + edge.astype(f32)).astype(bf)

    factor = 1.0 / math.sqrt(n_rows * places.n_lat * n_cols * places.n_lon)
    qkv_grad, out_grad, small = pl.pallas_call(
        functools.partial(unpack_kernel, counts, n_proj, factor),
        out_shape=(
            jax.ShapeDtypeStruct((n_chan, n_proj), f32),
            jax.ShapeDtypeStruct((n_chan, n_chan), f32),
            jax.ShapeDtypeStruct((n_chan, LANES), f32),
        ),
        in_specs=[smem] + [whole()] * 2,
        compiler_params=pltpu.CompilerParams(vmem_limit_bytes=32 * MIB),
        name="unpack",
    )(meta_inner, mine, other)
    bias_grad = jnp.concatenate([small[:n_head], small[n_head : 2 * n_head]], 1).reshape(n_head, 16, 16)
    span = 2 * WINDOW - 1
    return state_grad, qkv_grad, out_grad, small[:, LANES - 1], bias_grad[:, :span, :span].reshape(n_head, -1)


def solution(mesh):
    return jax.shard_map(
        local,
        mesh=mesh,
        in_specs=(P("lat", "lon", None), P("lat", "lon", None), P("lat"), P(), P(), P(), P(), P()),
        out_specs=(P("lat", "lon", None), P(), P(), P(), P()),
        check_vma=False,
    )
```

time: 308 us -> 157 us (0.51)
  blocking collectives: 177 us -> 0 us
  starting transfers between devices: 19 us -> 48.5 us
  waiting for transfers between devices: 8.26 us -> 36.1 us
  between operations: 18 us -> 0.92 us
  local copies, waits for them, and re-layouts: 33.6 us -> 19.2 us
  Pallas kernels: 31.7 us -> 41.1 us
  other arithmetic: 14.9 us -> 7.12 us
    psum x1 -> x0, blocking collectives: 87.8 us -> none  [local(): small = lax.psum(small, ('lat', 'lon')).reshape(-1) * norm_factor]
    all_to_all x2 -> x0, blocking collectives: 57.6 us -> none  [total_over_devices(): lax.all_to_all(array.astype(jnp.bfloat16).reshape(count, -1, array.shape[...]
    all_gather x1 -> x0, blocking collectives: 32 us -> none  [local(): lax.all_gather(part, 'lat', tiled=True)]
    ppermute x7 -> x22, starting transfers between devices: 19 us -> 48.5 us  [the longest x17 38.7 us: move(): return lax.ppermute(array, ('lat', 'lon'), pairs)]
    ppermute x7 -> x22, waiting for transfers between devices: 8.24 us -> 36.1 us  [the longest x17 30.2 us: move(): return lax.ppermute(array, ('lat', 'lon'), pairs)]
    dynamic_update_slice x1 -> x0, local copies, waits for them, and re-layouts: 10 us -> none  [local(): lax.dynamic_update_slice(ext_grad, grad_block, (shift_lat, shift_lon, zer...]
    pallas_call x2 -> x7, Pallas kernels: 31.7 us -> 41.1 us  [the longest x1 22.2 us: local(): pl.pallas_call(functools.partial(outer_kernel, n_head, counts), out_shape...]
    slice x10 -> x4, local copies, waits for them, and re-layouts: 8.87 us -> 0.93 us  [the longest x1 0.81 us: local(): small[:, LANES - 1]]
  transfers between devices with their start and end apart: 8 -> 22, of which waited for: 3 -> 13; matrix products, arithmetic and copies ran while one was open for 10% -> 8% of each run, Pallas kernels for 1% -> 10%
where the time goes in v2:
time: 157 us; the launch traced here: 154 us
  starting transfers between devices  48.5 us (31%)
  Pallas kernels  41.1 us (26%)
  waiting for transfers between devices  36.1 us (23%)
  local copies, waits for them, and re-layouts  19.2 us (12%)
  other arithmetic  7.12 us (5%)
    ppermute x17, starting transfers between devices, move(): return lax.ppermute(array, ('lat', 'lon'), pairs)  38.7 us
    ppermute x17, waiting for transfers between devices, move(): return lax.ppermute(array, ('lat', 'lon'), pairs)  30.2 us
    pallas_call x1, Pallas kernels, local(): pl.pallas_call(functools.partial(outer_kernel, n_head, counts), out_shape...  22.2 us
    unnamed x54, local copies, waits for them, and re-layouts  12.6 us
    pallas_call x1, Pallas kernels, local(): pl.pallas_call(functools.partial(inner_kernel, n_head), out_shape=(tile((...  11.9 us
    ppermute x5, starting transfers between devices, ring(): return lax.ppermute(array, ('lat', 'lon'), pairs)  9.85 us
    ppermute x5, waiting for transfers between devices, ring(): return lax.ppermute(array, ('lat', 'lon'), pairs)  5.97 us
    pallas_call x1, Pallas kernels, local(): pl.pallas_call(cells_kernel, out_shape=(tile((n_rows, n_cols, n_chan)), t...  3.75 us
  transfers between devices with their start and end apart: 22, of which 13 were waited for; matrix products, arithmetic and copies ran while one was open for 8% of the time, Pallas kernels for 10%

profile of v2, /device:TPU:1, one launch (start us, length us, event | category | flops | bytes accessed | tf_op | source)
XLA Modules:
  0.0 154.3 jit_solution(17881460255823358157)
XLA Ops:
  1.5 0.9 slice_bitcast_fusion.4
  3.1 5.2 %collective-permute-start = (bf16[3,8,8,512]{3,2,1,0:T(8,128)(2,1)}, bf16[3,8,8,512]{3,2,1,0:T(8,128)(2,1)}, u32[]{:S(2)}, u32[]{:S(2)}) collective-permute-start(bf16[3,8,8,512]{3,2,1,0:T(8,128)(2,1)} %pad_maximum_fusion.4), channel_id=1, source_target_pairs={{0,17},{1,18},{2,19},{3,20},{4,21},{5,22},{6,23},{7,24},{8,25},{9,... | collective-permute-start | bytes 589832 | tf_op jit(solution)/shard_map/ppermute | solution.py:364
  8.4 1.0 slice_bitcast_fusion.2
  10.1 1.1 slice_bitcast_fusion
  11.2 1.1 pad_maximum_fusion
  12.3 1.4 collective-permute-start.2
  13.9 1.3 convolution_bitcast_fusion
  15.2 1.0 reshape.115
  16.3 1.6 %copy.14 = bf16[512,1536]{0,1:T(8,128)(2,1)} copy(bf16[512,1536]{1,0:T(8,128)(2,1)S(1)} %copy-done.1) | data formatting | bytes 3145728 | tf_op args[5]
  17.9 1.5 pad_maximum_fusion.1.bias_ref
  19.4 1.0 fusion.1
  21.0 1.5 copy-done.6
  22.5 1.2 copy-done.12
  23.7 1.0 copy-done.16
  24.8 11.9 %inner.1 = (bf16[512,512]{1,0:T(8,128)(2,1)S(1)}, bf16[512,512]{1,0:T(8,128)(2,1)S(1)}, bf16[512,512]{1,0:T(8,128)(2,1)S(1)}, bf16[512,512]{1,0:T(8,128)(2,1)S(1...) custom-call(s32[29]{0:T(128)S(1)} %concatenate.25.meta, bf16[16,64,512]{2,1,0:T(8,128)(2,1)S(1)} %copy-done.12, ...), custom_call_target="tpu_custom_call" | custom-call | flops 8000000000 | bytes 16777216 | tf_op jit(solution)/shard_map/inner/pallas_call | solution.py:408
  36.7 1.2 copy-done.7
  38.6 0.8 copy-done.19
  39.5 0.9 copy-done.20
  41.2 1.6 %collective-permute-done.2.top_ref = bf16[2,8,64,512]{3,2,1,0:T(8,128)(2,1)} collective-permute-done((bf16[2,8,64,512]{3,2,1,0:T(8,128)(2,1)}, bf16[2,8,64,512]{3,2,1,0:T(8,128)(2,1)}, u32[]{:S(2)}, u32[]{:S(2)}) %collective-permute-start.2) | collective-permute-done | bytes 1048608 | tf_op jit(solution)/shard_map/ppermute | solution.py:364
  42.8 22.2 %outer.1 = (bf16[512,512]{1,0:T(8,128)(2,1)}, bf16[1536,512]{1,0:T(8,128)(2,1)}, f32[16,16,2176]{2,1,0:T(8,128)}, bf16[16,16,2176]{2,1,0:T(8,128)(2,1)}) custom-call(s32[29]{0:T(128)} %concatenate.24.meta, bf16[16,64,512]{2,1,0:T(8,128)(2,1)} %x_ref.3, bf16[16,64,512]{2,1,0:T(8,128)(2,1)} %cot_ref.5, bf16[2,16,8,512]{3,2,1,0:T(8,128)(2,1)} %copy-done.17, ...), custom_call_target="tpu_custom_call" | custom-call | flops 10000000000 | bytes 25165824 | tf_op jit(solution)/shard_map/outer/pallas_call | solution.py:430
  65.0 0.8 collective-permute-start.5
  65.8 2.6 %collective-permute-done.5.got_ref = bf16[16,16,2176]{2,1,0:T(8,128)(2,1)S(1)} collective-permute-done((bf16[16,16,2176]{2,1,0:T(8,128)(2,1)}, bf16[16,16,2176]{2,1,0:T(8,128)(2,1)S(1)}, u32[]{:S(2)}, u32[]{:S(2)}) %collective-permute-start.5) | collective-permute-done | bytes 1114144 | tf_op jit(solution)/shard_map/ppermute | solution.py:314
  68.4 1.6 %copy-done.5 = f32[16,16,2176]{2,1,0:T(8,128)S(1)} copy-done((f32[16,16,2176]{2,1,0:T(8,128)S(1)}, f32[16,16,2176]{2,1,0:T(8,128)}, u32[]{:S(2)}) %copy-start.5) | copy-done | bytes 2228248
  70.5 2.2 %collective-permute-start.7 = (bf16[4,16,2176]{2,1,0:T(8,128)(2,1)S(1)}, bf16[4,16,2176]{2,1,0:T(8,128)(2,1)S(1)}, u32[]{:S(2)}, u32[]{:S(2)}) collective-permute-start(bf16[4,16,2176]{2,1,0:T(8,128)(2,1)S(1)} %get-tuple-element.44), channel_id=1, source_target_pairs={{0,4},{1,5},{2,6},{3,7},{4,0},{5,1},{6,2},{7,3},{8,12},{9,13},{10,... | collective-permute-start | bytes 835592 | tf_op jit(solution)/shard_map/ppermute | solution.py:314
  72.7 1.0 collective-permute-start.8
  73.7 6.2 %collective-permute-done.6.refs_0_ = bf16[4,16,2176]{2,1,0:T(8,128)(2,1)S(1)} collective-permute-done((bf16[4,16,2176]{2,1,0:T(8,128)(2,1)S(1)}, bf16[4,16,2176]{2,1,0:T(8,128)(2,1)S(1)}, u32[]{:S(2)}, u32[]{:S(2)}) %collective-permute-start.6) | collective-permute-done | bytes 278560 | tf_op jit(solution)/shard_map/ppermute | solution.py:314
  79.9 5.5 %collective-permute-done.7.refs_1_ = bf16[4,16,2176]{2,1,0:T(8,128)(2,1)S(1)} collective-permute-done((bf16[4,16,2176]{2,1,0:T(8,128)(2,1)S(1)}, bf16[4,16,2176]{2,1,0:T(8,128)(2,1)S(1)}, u32[]{:S(2)}, u32[]{:S(2)}) %collective-permute-start.7) | collective-permute-done | bytes 278560 | tf_op jit(solution)/shard_map/ppermute | solution.py:314
  86.1 2.5 %collective-permute-start.10 = (bf16[1,16,2176]{2,1,0:T(8,128)(2,1)S(1)}, bf16[1,16,2176]{2,1,0:T(8,128)(2,1)S(1)}, u32[]{:S(2)}, u32[]{:S(2)}) collective-permute-start(bf16[1,16,2176]{2,1,0:T(8,128)(2,1)S(1)} %get-tuple-element.48), channel_id=1, source_target_pairs={{0,16},{1,17},{2,18},{3,19},{4,20},{5,21},{6,22},{7,23},{8,24},{9,... | collective-permute-start | bytes 208904 | tf_op jit(solution)/shard_map/ppermute | solution.py:314
  89.4 1.8 %collective-permute-done.9.refs_0_ = bf16[1,16,2176]{2,1,0:T(8,128)(2,1)S(1)} collective-permute-done((bf16[1,16,2176]{2,1,0:T(8,128)(2,1)S(1)}, bf16[1,16,2176]{2,1,0:T(8,128)(2,1)S(1)}, u32[]{:S(2)}, u32[]{:S(2)}) %collective-permute-start.9) | collective-permute-done | bytes 69664 | tf_op jit(solution)/shard_map/ppermute | solution.py:314
  91.2 0.9 collective-permute-done.11.refs_2_
  92.1 2.2 %collective-permute-start.12 = (bf16[1,16,2176]{2,1,0:T(8,128)(2,1)S(1)}, bf16[1,16,2176]{2,1,0:T(8,128)(2,1)S(1)}, u32[]{:S(2)}, u32[]{:S(2)}) collective-permute-start(bf16[1,16,2176]{2,1,0:T(8,128)(2,1)S(1)} %add_y.1), channel_id=1, source_target_pairs={{0,32},{1,33},{2,34},{3,35},{4,36},{5,37},{6,38},{7,39},{8,40},{9,... | collective-permute-start | bytes 208904 | tf_op jit(solution)/shard_map/ppermute | solution.py:314
  94.3 1.7 %collective-permute-done.12 = bf16[1,16,2176]{2,1,0:T(8,128)(2,1)S(1)} collective-permute-done((bf16[1,16,2176]{2,1,0:T(8,128)(2,1)S(1)}, bf16[1,16,2176]{2,1,0:T(8,128)(2,1)S(1)}, u32[]{:S(2)}, u32[]{:S(2)}) %collective-permute-start.12) | collective-permute-done | bytes 69664 | tf_op jit(solution)/shard_map/ppermute | solution.py:314
  96.0 4.3 %collective-permute-start.13 = (bf16[1,16,2176]{2,1,0:T(8,128)(2,1)S(1)}, bf16[1,16,2176]{2,1,0:T(8,128)(2,1)S(1)}, u32[]{:S(2)}, u32[]{:S(2)}) collective-permute-start(bf16[1,16,2176]{2,1,0:T(8,128)(2,1)S(1)} %add_convert_fusion.3), channel_id=1, source_target_pairs={{0,64},{1,65},{2,66},{3,67},{4,68},{5,69},{6,70},{7,71},{8,72},{9,... | collective-permute-start | bytes 208904 | tf_op jit(solution)/shard_map/ppermute | solution.py:314
  100.3 1.7 %collective-permute-done.13 = bf16[1,16,2176]{2,1,0:T(8,128)(2,1)S(1)} collective-permute-done((bf16[1,16,2176]{2,1,0:T(8,128)(2,1)S(1)}, bf16[1,16,2176]{2,1,0:T(8,128)(2,1)S(1)}, u32[]{:S(2)}, u32[]{:S(2)}) %collective-permute-start.13) | collective-permute-done | bytes 69664 | tf_op jit(solution)/shard_map/ppermute | solution.py:314
  102.0 3.2 %collective-permute-start.14 = (bf16[1,16,2176]{2,1,0:T(8,128)(2,1)S(1)}, bf16[1,16,2176]{2,1,0:T(8,128)(2,1)S(1)}, u32[]{:S(2)}, u32[]{:S(2)}) collective-permute-start(bf16[1,16,2176]{2,1,0:T(8,128)(2,1)S(1)} %add_convert_fusion.2), channel_id=1, source_target_pairs={{0,192},{1,193},{2,194},{3,195},{4,196},{5,197},{6,198},{7,199},{8... | collective-permute-start | bytes 208904 | tf_op jit(solution)/shard_map/ppermute | solution.py:314
  105.2 2.8 %collective-permute-done.14 = bf16[1,16,2176]{2,1,0:T(8,128)(2,1)S(1)} collective-permute-done((bf16[1,16,2176]{2,1,0:T(8,128)(2,1)S(1)}, bf16[1,16,2176]{2,1,0:T(8,128)(2,1)S(1)}, u32[]{:S(2)}, u32[]{:S(2)}) %collective-permute-start.14) | collective-permute-done | bytes 69664 | tf_op jit(solution)/shard_map/ppermute | solution.py:314
  108.2 2.0 %collective-permute-start.16 = (bf16[1,16,2176]{2,1,0:T(8,128)(2,1)S(1)}, bf16[1,16,2176]{2,1,0:T(8,128)(2,1)S(1)}, u32[]{:S(2)}, u32[]{:S(2)}) collective-permute-start(bf16[1,16,2176]{2,1,0:T(8,128)(2,1)S(1)} %get-tuple-element.54), channel_id=1, source_target_pairs={{0,16},{1,17},{2,18},{3,19},{4,20},{5,21},{6,22},{7,23},{8,24},{9,... | collective-permute-start | bytes 208904 | tf_op jit(solution)/shard_map/ppermute | solution.py:314
  110.2 1.0 collective-permute-start.15
  111.2 1.0 copy-done.10
  112.2 3.7 %cells.1 = (bf16[16,64,512]{2,1,0:T(8,128)(2,1)S(1)}, bf16[8,72,512]{2,1,0:T(8,128)(2,1)S(1)}, bf16[16,8,512]{2,1,0:T(8,128)(2,1)S(1)}) custom-call(s32[29]{0:T(128)S(1)} %copy-done.15, bf16[512,512]{1,0:T(8,128)(2,1)S(1)} %get-tuple-element.29.xa_ref, bf16[512,512]{1,0:T(8,128)(2,1)S(1)} %copy-done.10, bf16[1536,512]{1,0:T(8,128)(2,1)S(1)} %copy-done.8, ...), custom_call_target="tpu_custom_call" | custom-call | flops 1600000000 | bytes 12582912 | tf_op jit(solution)/shard_map/cells/pallas_call | solution.py:456
  116.0 3.1 %collective-permute-start.3 = (bf16[8,72,512]{2,1,0:T(8,128)(2,1)S(1)}, bf16[8,72,512]{2,1,0:T(8,128)(2,1)S(1)}, u32[]{:S(2)}, u32[]{:S(2)}) collective-permute-start(bf16[8,72,512]{2,1,0:T(8,128)(2,1)S(1)} %get-tuple-element.38), channel_id=1, source_target_pairs={{0,240},{1,241},{2,242},{3,243},{4,244},{5,245},{6,246},{7,247},{8... | collective-permute-start | bytes 1769480 | tf_op jit(solution)/shard_map/ppermute | solution.py:364
  119.2 1.9 %collective-permute-start.20 = (bf16[4,16,2176]{2,1,0:T(8,128)(2,1)S(1)}, bf16[4,16,2176]{2,1,0:T(8,128)(2,1)S(1)}, u32[]{:S(2)}, u32[]{:S(2)}) collective-permute-start(bf16[4,16,2176]{2,1,0:T(8,128)(2,1)S(1)} %pad_maximum_fusion.2), channel_id=1, source_target_pairs={{0,2},{1,3},{2,4},{3,5},{4,6},{5,7},{6,0},{7,1},{8,10},{9,11},{10,... | collective-permute-start | bytes 835592 | tf_op jit(solution)/shard_map/ppermute | solution.py:314
  121.1 2.1 %collective-permute-start.19 = (bf16[4,16,2176]{2,1,0:T(8,128)(2,1)S(1)}, bf16[4,16,2176]{2,1,0:T(8,128)(2,1)S(1)}, u32[]{:S(2)}, u32[]{:S(2)}) collective-permute-start(bf16[4,16,2176]{2,1,0:T(8,128)(2,1)S(1)} %pad_maximum_fusion.2), channel_id=1, source_target_pairs={{0,4},{1,5},{2,6},{3,7},{4,0},{5,1},{6,2},{7,3},{8,12},{9,13},{10,... | collective-permute-start | bytes 835592 | tf_op jit(solution)/shard_map/ppermute | solution.py:314
  123.9 6.3 %collective-permute-done.18 = bf16[4,16,2176]{2,1,0:T(8,128)(2,1)S(1)} collective-permute-done((bf16[4,16,2176]{2,1,0:T(8,128)(2,1)S(1)}, bf16[4,16,2176]{2,1,0:T(8,128)(2,1)S(1)}, u32[]{:S(2)}, u32[]{:S(2)}) %collective-permute-start.18) | collective-permute-done | bytes 278560 | tf_op jit(solution)/shard_map/ppermute | solution.py:314
  130.5 13.6 %collective-permute-start.21 = (bf16[16,16,2176]{2,1,0:T(8,128)(2,1)S(1)}, bf16[16,16,2176]{2,1,0:T(8,128)(2,1)S(1)}, u32[]{:S(2)}, u32[]{:S(2)}) collective-permute-start(bf16[16,16,2176]{2,1,0:T(8,128)(2,1)S(1)} %constant_dynamic-update-slice_fusion.mine_ref), channel_id=1, source_target_pairs={{0,1},{1,0},{2,3},{3,2},{4,5},{5,4},{6,7},{7,6},{8,9},{9,8},{10,11... | collective-permute-start | bytes 3342344 | tf_op jit(solution)/shard_map/ppermute | solution.py:314
  144.3 4.3 %collective-permute-done.4 = bf16[16,8,512]{2,1,0:T(8,128)(2,1)S(1)} collective-permute-done((bf16[16,8,512]{2,1,0:T(8,128)(2,1)S(1)}, bf16[16,8,512]{2,1,0:T(8,128)(2,1)S(1)}, u32[]{:S(2)}, u32[]{:S(2)}) %collective-permute-start.4) | collective-permute-done | bytes 131104 | tf_op jit(solution)/shard_map/ppermute | solution.py:364
  148.6 1.2 add_convert_fusion
  149.8 2.9 %unpack.1 = (f32[512,1536]{1,0:T(8,128)}, f32[512,512]{1,0:T(8,128)}, f32[512,128]{1,0:T(8,128)S(1)}) custom-call(s32[29]{0:T(128)S(1)} %concatenate.25.meta, bf16[16,16,2176]{2,1,0:T(8,128)(2,1)S(1)} %constant_dynamic-update-slice_fusion.mine_ref, bf16[16,16,2176]{2,1,0:T(8,128)(2,1)S(1)} %collective-permute-done.21.other_ref), custom_call_target="tpu_custom_call" | custom-call | tf_op jit(solution)/shard_map/unpack/pallas_call | solution.py:477
  (90 shorter events, 9.9 us)
Async XLA Ops:
  0.6 13.3 %copy-start = (f32[16,225]{1,0:T(8,128)S(1)}, f32[16,225]{1,0:T(8,128)}, u32[]{:S(2)}) copy-start(f32[16,225]{1,0:T(8,128)} %param.15) | copy-start | bytes 43204
  0.6 9.5 %copy-start.3 = (bf16[16,64,512]{2,1,0:T(8,128)(2,1)S(1)}, bf16[16,64,512]{2,1,0:T(8,128)(2,1)}, u32[]{:S(2)}) copy-start(bf16[16,64,512]{2,1,0:T(8,128)(2,1)} %cot_ref.5) | copy-start | bytes 3145732
  3.1 16.2 %collective-permute-start = (bf16[3,8,8,512]{3,2,1,0:T(8,128)(2,1)}, bf16[3,8,8,512]{3,2,1,0:T(8,128)(2,1)}, u32[]{:S(2)}, u32[]{:S(2)}) collective-permute-start(bf16[3,8,8,512]{3,2,1,0:T(8,128)(2,1)} %pad_maximum_fusion.4), channel_id=1, source_target_pairs={{0,17},{1,18},{2,19},{3,20},{4,21},{5,22},{6,23},{7,24},{8,25},{9,... | collective-permute-start | bytes 589832 | tf_op jit(solution)/shard_map/ppermute | solution.py:364
  10.1 10.9 %collective-permute-start.1 = (bf16[2,16,8,512]{3,2,1,0:T(8,128)(2,1)}, bf16[2,16,8,512]{3,2,1,0:T(8,128)(2,1)S(1)}, u32[]{:S(2)}, u32[]{:S(2)}) collective-permute-start(bf16[2,16,8,512]{3,2,1,0:T(8,128)(2,1)} %pad_maximum_fusion.3), channel_id=1, source_target_pairs={{0,1},{1,2},{2,3},{3,4},{4,5},{5,6},{6,7},{7,8},{8,9},{9,10},{10,1... | collective-permute-start | bytes 786440 | tf_op jit(solution)/shard_map/ppermute | solution.py:364
  12.3 4.0 %copy-start.1 = (bf16[512,1536]{1,0:T(8,128)(2,1)S(1)}, bf16[512,1536]{1,0:T(8,128)(2,1)}, u32[]{:S(2)}) copy-start(bf16[512,1536]{1,0:T(8,128)(2,1)} %w_ref.5) | copy-start | bytes 4718596
  12.3 30.5 %collective-permute-start.2 = (bf16[2,8,64,512]{3,2,1,0:T(8,128)(2,1)}, bf16[2,8,64,512]{3,2,1,0:T(8,128)(2,1)}, u32[]{:S(2)}, u32[]{:S(2)}) collective-permute-start(bf16[2,8,64,512]{3,2,1,0:T(8,128)(2,1)} %pad_maximum_fusion), channel_id=1, source_target_pairs={{0,16},{1,17},{2,18},{3,19},{4,20},{5,21},{6,22},{7,23},{8,24},{9,... | collective-permute-start | bytes 3145736 | tf_op jit(solution)/shard_map/ppermute | solution.py:364
  16.3 1.6 %copy-start.22 = (s32[2]{0:T(128)S(1)}, s32[2]{0:T(128)}, u32[]{:S(2)}) copy-start(s32[2]{0:T(128)} %param.11) | copy-start | bytes 28
  16.3 1.6 %copy-start.23 = (s32[16]{0:T(128)S(1)}, s32[16]{0:T(128)}, u32[]{:S(2)}) copy-start(s32[16]{0:T(128)} %param.10) | copy-start | bytes 196
  16.3 4.7 %copy-start.13 = (f32[512]{0:T(512)S(1)}, f32[512]{0:T(512)}, u32[]{:S(2)}) copy-start(f32[512]{0:T(512)} %param.12) | copy-start | bytes 6148
  19.4 17.3 %copy-start.11 = (f32[16,64,128]{2,1,0:T(8,128)}, f32[16,64,128]{2,1,0:T(8,128)S(1)}, u32[]{:S(2)}) copy-start(f32[16,64,128]{2,1,0:T(8,128)S(1)} %pad_maximum_fusion.1.bias_ref) | copy-start | bytes 1572868
  21.0 15.7 %copy-start.17 = (bf16[2,16,8,512]{3,2,1,0:T(8,128)(2,1)}, bf16[2,16,8,512]{3,2,1,0:T(8,128)(2,1)S(1)}, u32[]{:S(2)}) copy-start(bf16[2,16,8,512]{3,2,1,0:T(8,128)(2,1)S(1)} %collective-permute-done.1.side_ref) | copy-start | bytes 786436
  21.0 1.5 copy-start.6
  22.5 1.2 copy-start.12
  23.7 1.0 copy-start.16
  36.7 1.2 copy-start.7
  37.9 0.8 copy-start.18
  38.6 0.9 copy-start.19
  39.5 0.9 copy-start.20
  40.4 0.8 copy-start.21
  65.0 3.4 %collective-permute-start.5 = (bf16[16,16,2176]{2,1,0:T(8,128)(2,1)}, bf16[16,16,2176]{2,1,0:T(8,128)(2,1)S(1)}, u32[]{:S(2)}, u32[]{:S(2)}) collective-permute-start(bf16[16,16,2176]{2,1,0:T(8,128)(2,1)} %get-tuple-element.41), channel_id=1, source_target_pairs={{0,1},{1,0},{2,3},{3,2},{4,5},{5,4},{6,7},{7,6},{8,9},{9,8},{10,11... | collective-permute-start | bytes 3342344 | tf_op jit(solution)/shard_map/ppermute | solution.py:314
  68.4 1.6 %copy-start.5 = (f32[16,16,2176]{2,1,0:T(8,128)S(1)}, f32[16,16,2176]{2,1,0:T(8,128)}, u32[]{:S(2)}) copy-start(f32[16,16,2176]{2,1,0:T(8,128)} %get-tuple-element.40.keep_ref) | copy-start | bytes 6684676
  70.0 41.1 %copy-start.4 = (bf16[16,64,512]{2,1,0:T(8,128)(2,1)S(1)}, bf16[16,64,512]{2,1,0:T(8,128)(2,1)}, u32[]{:S(2)}) copy-start(bf16[16,64,512]{2,1,0:T(8,128)(2,1)} %cot_ref.5) | copy-start | bytes 3145732
  70.0 41.1 %copy-start.8 = (bf16[1536,512]{1,0:T(8,128)(2,1)S(1)}, bf16[1536,512]{1,0:T(8,128)(2,1)}, u32[]{:S(2)}) copy-start(bf16[1536,512]{1,0:T(8,128)(2,1)} %copy-done.7) | copy-start | bytes 4718596
  70.0 41.1 %copy-start.9 = (bf16[1536,512]{1,0:T(8,128)(2,1)S(1)}, bf16[1536,512]{1,0:T(8,128)(2,1)}, u32[]{:S(2)}) copy-start(bf16[1536,512]{1,0:T(8,128)(2,1)} %get-tuple-element.36.gpb_ref) | copy-start | bytes 4718596
  70.2 9.6 %collective-permute-start.6 = (bf16[4,16,2176]{2,1,0:T(8,128)(2,1)S(1)}, bf16[4,16,2176]{2,1,0:T(8,128)(2,1)S(1)}, u32[]{:S(2)}, u32[]{:S(2)}) collective-permute-start(bf16[4,16,2176]{2,1,0:T(8,128)(2,1)S(1)} %get-tuple-element.43), channel_id=1, source_target_pairs={{0,2},{1,3},{2,4},{3,5},{4,6},{5,7},{6,0},{7,1},{8,10},{9,11},{10,... | collective-permute-start | bytes 835592 | tf_op jit(solution)/shard_map/ppermute | solution.py:314
  70.5 14.8 %collective-permute-start.7 = (bf16[4,16,2176]{2,1,0:T(8,128)(2,1)S(1)}, bf16[4,16,2176]{2,1,0:T(8,128)(2,1)S(1)}, u32[]{:S(2)}, u32[]{:S(2)}) collective-permute-start(bf16[4,16,2176]{2,1,0:T(8,128)(2,1)S(1)} %get-tuple-element.44), channel_id=1, source_target_pairs={{0,4},{1,5},{2,6},{3,7},{4,0},{5,1},{6,2},{7,3},{8,12},{9,13},{10,... | collective-permute-start | bytes 835592 | tf_op jit(solution)/shard_map/ppermute | solution.py:314
  72.7 13.2 %collective-permute-start.8 = (bf16[4,16,2176]{2,1,0:T(8,128)(2,1)S(1)}, bf16[4,16,2176]{2,1,0:T(8,128)(2,1)S(1)}, u32[]{:S(2)}, u32[]{:S(2)}) collective-permute-start(bf16[4,16,2176]{2,1,0:T(8,128)(2,1)S(1)} %get-tuple-element.45), channel_id=1, source_target_pairs={{0,6},{1,7},{2,0},{3,1},{4,2},{5,3},{6,4},{7,5},{8,14},{9,15},{10,... | collective-permute-start | bytes 835592 | tf_op jit(solution)/shard_map/ppermute | solution.py:314
  85.9 25.3 %copy-start.2 = (bf16[512,1536]{1,0:T(8,128)(2,1)S(1)}, bf16[512,1536]{1,0:T(8,128)(2,1)}, u32[]{:S(2)}) copy-start(bf16[512,1536]{1,0:T(8,128)(2,1)} %w_ref.5) | copy-start | bytes 4718596
  85.9 25.3 %copy-start.14 = (f32[512]{0:T(512)S(1)}, f32[512]{0:T(512)}, u32[]{:S(2)}) copy-start(f32[512]{0:T(512)} %param.12) | copy-start | bytes 6148
  85.9 25.3 %copy-start.15 = (s32[29]{0:T(128)S(1)}, s32[29]{0:T(128)}, u32[]{:S(2)}) copy-start(s32[29]{0:T(128)} %concatenate.24.meta) | copy-start | bytes 352
  86.0 5.2 %collective-permute-start.9 = (bf16[1,16,2176]{2,1,0:T(8,128)(2,1)S(1)}, bf16[1,16,2176]{2,1,0:T(8,128)(2,1)S(1)}, u32[]{:S(2)}, u32[]{:S(2)}) collective-permute-start(bf16[1,16,2176]{2,1,0:T(8,128)(2,1)S(1)} %get-tuple-element.47), channel_id=1, source_target_pairs={{0,8},{1,9},{2,10},{3,11},{4,12},{5,13},{6,14},{7,15},{8,16},{9,17... | collective-permute-start | bytes 208904 | tf_op jit(solution)/shard_map/ppermute | solution.py:314
  86.1 5.1 %collective-permute-start.10 = (bf16[1,16,2176]{2,1,0:T(8,128)(2,1)S(1)}, bf16[1,16,2176]{2,1,0:T(8,128)(2,1)S(1)}, u32[]{:S(2)}, u32[]{:S(2)}) collective-permute-start(bf16[1,16,2176]{2,1,0:T(8,128)(2,1)S(1)} %get-tuple-element.48), channel_id=1, source_target_pairs={{0,16},{1,17},{2,18},{3,19},{4,20},{5,21},{6,22},{7,23},{8,24},{9,... | collective-permute-start | bytes 208904 | tf_op jit(solution)/shard_map/ppermute | solution.py:314
  88.6 3.5 %collective-permute-start.11 = (bf16[1,16,2176]{2,1,0:T(8,128)(2,1)S(1)}, bf16[1,16,2176]{2,1,0:T(8,128)(2,1)S(1)}, u32[]{:S(2)}, u32[]{:S(2)}) collective-permute-start(bf16[1,16,2176]{2,1,0:T(8,128)(2,1)S(1)} %get-tuple-element.49), channel_id=1, source_target_pairs={{0,24},{1,25},{2,26},{3,27},{4,28},{5,29},{6,30},{7,31},{8,0},{9,1... | collective-permute-start | bytes 208904 | tf_op jit(solution)/shard_map/ppermute | solution.py:314
  92.1 3.9 %collective-permute-start.12 = (bf16[1,16,2176]{2,1,0:T(8,128)(2,1)S(1)}, bf16[1,16,2176]{2,1,0:T(8,128)(2,1)S(1)}, u32[]{:S(2)}, u32[]{:S(2)}) collective-permute-start(bf16[1,16,2176]{2,1,0:T(8,128)(2,1)S(1)} %add_y.1), channel_id=1, source_target_pairs={{0,32},{1,33},{2,34},{3,35},{4,36},{5,37},{6,38},{7,39},{8,40},{9,... | collective-permute-start | bytes 208904 | tf_op jit(solution)/shard_map/ppermute | solution.py:314
  96.0 6.0 %collective-permute-start.13 = (bf16[1,16,2176]{2,1,0:T(8,128)(2,1)S(1)}, bf16[1,16,2176]{2,1,0:T(8,128)(2,1)S(1)}, u32[]{:S(2)}, u32[]{:S(2)}) collective-permute-start(bf16[1,16,2176]{2,1,0:T(8,128)(2,1)S(1)} %add_convert_fusion.3), channel_id=1, source_target_pairs={{0,64},{1,65},{2,66},{3,67},{4,68},{5,69},{6,70},{7,71},{8,72},{9,... | collective-permute-start | bytes 208904 | tf_op jit(solution)/shard_map/ppermute | solution.py:314
  102.0 6.0 %collective-permute-start.14 = (bf16[1,16,2176]{2,1,0:T(8,128)(2,1)S(1)}, bf16[1,16,2176]{2,1,0:T(8,128)(2,1)S(1)}, u32[]{:S(2)}, u32[]{:S(2)}) collective-permute-start(bf16[1,16,2176]{2,1,0:T(8,128)(2,1)S(1)} %add_convert_fusion.2), channel_id=1, source_target_pairs={{0,192},{1,193},{2,194},{3,195},{4,196},{5,197},{6,198},{7,199},{8... | collective-permute-start | bytes 208904 | tf_op jit(solution)/shard_map/ppermute | solution.py:314
  108.0 11.1 %collective-permute-start.17 = (bf16[1,16,2176]{2,1,0:T(8,128)(2,1)S(1)}, bf16[1,16,2176]{2,1,0:T(8,128)(2,1)S(1)}, u32[]{:S(2)}, u32[]{:S(2)}) collective-permute-start(bf16[1,16,2176]{2,1,0:T(8,128)(2,1)S(1)} %get-tuple-element.54), channel_id=1, source_target_pairs={{0,8},{1,9},{2,10},{3,11},{4,12},{5,13},{6,14},{7,15},{8,16},{9,17... | collective-permute-start | bytes 208904 | tf_op jit(solution)/shard_map/ppermute | solution.py:314
  108.2 10.9 %collective-permute-start.16 = (bf16[1,16,2176]{2,1,0:T(8,128)(2,1)S(1)}, bf16[1,16,2176]{2,1,0:T(8,128)(2,1)S(1)}, u32[]{:S(2)}, u32[]{:S(2)}) collective-permute-start(bf16[1,16,2176]{2,1,0:T(8,128)(2,1)S(1)} %get-tuple-element.54), channel_id=1, source_target_pairs={{0,16},{1,17},{2,18},{3,19},{4,20},{5,21},{6,22},{7,23},{8,24},{9,... | collective-permute-start | bytes 208904 | tf_op jit(solution)/shard_map/ppermute | solution.py:314
  110.2 9.0 %collective-permute-start.15 = (bf16[1,16,2176]{2,1,0:T(8,128)(2,1)S(1)}, bf16[1,16,2176]{2,1,0:T(8,128)(2,1)S(1)}, u32[]{:S(2)}, u32[]{:S(2)}) collective-permute-start(bf16[1,16,2176]{2,1,0:T(8,128)(2,1)S(1)} %get-tuple-element.54), channel_id=1, source_target_pairs={{0,24},{1,25},{2,26},{3,27},{4,28},{5,29},{6,30},{7,31},{8,0},{9,1... | collective-permute-start | bytes 208904 | tf_op jit(solution)/shard_map/ppermute | solution.py:314
  111.2 1.0 copy-start.10
  116.0 28.1 %collective-permute-start.3 = (bf16[8,72,512]{2,1,0:T(8,128)(2,1)S(1)}, bf16[8,72,512]{2,1,0:T(8,128)(2,1)S(1)}, u32[]{:S(2)}, u32[]{:S(2)}) collective-permute-start(bf16[8,72,512]{2,1,0:T(8,128)(2,1)S(1)} %get-tuple-element.38), channel_id=1, source_target_pairs={{0,240},{1,241},{2,242},{3,243},{4,244},{5,245},{6,246},{7,247},{8... | collective-permute-start | bytes 1769480 | tf_op jit(solution)/shard_map/ppermute | solution.py:364
  119.2 11.3 %collective-permute-start.20 = (bf16[4,16,2176]{2,1,0:T(8,128)(2,1)S(1)}, bf16[4,16,2176]{2,1,0:T(8,128)(2,1)S(1)}, u32[]{:S(2)}, u32[]{:S(2)}) collective-permute-start(bf16[4,16,2176]{2,1,0:T(8,128)(2,1)S(1)} %pad_maximum_fusion.2), channel_id=1, source_target_pairs={{0,2},{1,3},{2,4},{3,5},{4,6},{5,7},{6,0},{7,1},{8,10},{9,11},{10,... | collective-permute-start | bytes 835592 | tf_op jit(solution)/shard_map/ppermute | solution.py:314
  121.1 9.3 %collective-permute-start.19 = (bf16[4,16,2176]{2,1,0:T(8,128)(2,1)S(1)}, bf16[4,16,2176]{2,1,0:T(8,128)(2,1)S(1)}, u32[]{:S(2)}, u32[]{:S(2)}) collective-permute-start(bf16[4,16,2176]{2,1,0:T(8,128)(2,1)S(1)} %pad_maximum_fusion.2), channel_id=1, source_target_pairs={{0,4},{1,5},{2,6},{3,7},{4,0},{5,1},{6,2},{7,3},{8,12},{9,13},{10,... | collective-permute-start | bytes 835592 | tf_op jit(solution)/shard_map/ppermute | solution.py:314
  123.2 7.0 %collective-permute-start.18 = (bf16[4,16,2176]{2,1,0:T(8,128)(2,1)S(1)}, bf16[4,16,2176]{2,1,0:T(8,128)(2,1)S(1)}, u32[]{:S(2)}, u32[]{:S(2)}) collective-permute-start(bf16[4,16,2176]{2,1,0:T(8,128)(2,1)S(1)} %pad_maximum_fusion.2), channel_id=1, source_target_pairs={{0,6},{1,7},{2,0},{3,1},{4,2},{5,3},{6,4},{7,5},{8,14},{9,15},{10,... | collective-permute-start | bytes 835592 | tf_op jit(solution)/shard_map/ppermute | solution.py:314
  130.5 19.3 %collective-permute-start.21 = (bf16[16,16,2176]{2,1,0:T(8,128)(2,1)S(1)}, bf16[16,16,2176]{2,1,0:T(8,128)(2,1)S(1)}, u32[]{:S(2)}, u32[]{:S(2)}) collective-permute-start(bf16[16,16,2176]{2,1,0:T(8,128)(2,1)S(1)} %constant_dynamic-update-slice_fusion.mine_ref), channel_id=1, source_target_pairs={{0,1},{1,0},{2,3},{3,2},{4,5},{5,4},{6,7},{7,6},{8,9},{9,8},{10,11... | collective-permute-start | bytes 3342344 | tf_op jit(solution)/shard_map/ppermute | solution.py:314
  144.1 4.5 %collective-permute-start.4 = (bf16[16,8,512]{2,1,0:T(8,128)(2,1)S(1)}, bf16[16,8,512]{2,1,0:T(8,128)(2,1)S(1)}, u32[]{:S(2)}, u32[]{:S(2)}) collective-permute-start(bf16[16,8,512]{2,1,0:T(8,128)(2,1)S(1)} %pad_maximum_fusion.5), channel_id=1, source_target_pairs={{0,15},{1,0},{2,1},{3,2},{4,3},{5,4},{6,5},{7,6},{8,7},{9,8},{10,9... | collective-permute-start | bytes 393224 | tf_op jit(solution)/shard_map/ppermute | solution.py:364
